TPU v7x, 256 devices: a whole 4x4x8 slice. The times are simulated.
256 devices in a mesh: src: 32 (over y, z), tgt: 8 (over x, core).
Axes of the slice: x: 4, y: 4, z: 8, core: 2. Of those that a mesh axis runs over, the one named last changes fastest.
Arguments:
- source_points: bfloat16 [131072, 64], P('src'), may hold values from -4 to 4
- target_points: bfloat16 [262144, 64], P('tgt'), may hold values from -4 to 4
- tile_lists: int32 [512, 8, 4], P('src', 'tgt'), may hold values from 0 to 127, as said below
- tile_counts: int32 [512, 8], P('src', 'tgt'), may hold values from 1 to 4, as said below
Outputs:
- source_potential: float32 [131072], P('src')
- target_potential: float32 [262144], P('tgt')
Inputs may be any that keep to these rules, and one draw needn't show every extreme that they name: `tile_lists`: the entries of one list are distinct; entries at slots k >= the count are valid numbers but not live; every target tile is live in some list. `tile_counts`: the largest count is 4 in every draw.
All inputs are finite; a program needn't handle non-finite values.
Results may differ from a plain program's by a relative error of at most 0.0003.
Values sent between devices are 32-bit elements; how exact they have to be, the bound alone decides.
No kernel may reach another device: no remote copies, remote signals or barrier semaphores. Data moves between devices by JAX's collectives and lax.ppermute only.
A program may use at most 128 MiB of HBM per device.

v0:
```python
import math

import jax
import jax.numpy as jnp
from jax import lax
from jax.sharding import PartitionSpec as P

TILE = 256
E = 64
KLOC = 4
ITERS = 4


epsilon = 1.0
lowest = -1e30


def joined(value, axis, join):
    pieces = jax.tree.map(lambda part: lax.all_gather(part, axis), value)
    head = jax.tree.map(lambda part: part[0], pieces)
    tail = jax.tree.map(lambda part: part[1:], pieces)
    total, _ = lax.scan(lambda total, piece: (join(total, piece), None), head, tail)
    return total


def combine_stats(first, second):
    peak = jnp.maximum(first[0], second[0])
    return (peak, first[1] * jnp.exp(first[0] - peak) + second[1] * jnp.exp(second[0] - peak))


def local(source_points, target_points, tile_lists, tile_counts):
    source_count = source_points.shape[0] // TILE
    target_count = target_points.shape[0] // TILE
    group = math.gcd(source_count, max(1, 2048 // TILE))
    blocks = source_count // group
    source_tiles = source_points.reshape(source_count, TILE, E)
    target_tiles = target_points.reshape(target_count, TILE, E)
    source_norm = 0.5 * jnp.sum(jnp.square(source_tiles.astype(jnp.float32)), -1)
    target_norm = 0.5 * jnp.sum(jnp.square(target_tiles.astype(jnp.float32)), -1)
    local_lists = tile_lists[:, 0, :]
    usable_all = jnp.arange(KLOC, dtype=jnp.int32)[None, :] < tile_counts[:, 0][:, None]
    picked_tiles = target_tiles[local_lists]
    picked_norms = target_norm[local_lists]
    log_source = -jnp.log(jnp.float32(source_points.shape[0] * lax.axis_size("src")))
    log_target = -jnp.log(jnp.float32(target_points.shape[0] * lax.axis_size("tgt")))
    scanned = (
        source_tiles.reshape(blocks, group, TILE, E),
        source_norm.reshape(blocks, group, TILE),
        local_lists.reshape(blocks, group, KLOC),
        usable_all.reshape(blocks, group, KLOC),
        picked_tiles.reshape(blocks, group, KLOC, TILE, E),
        picked_norms.reshape(blocks, group, KLOC, TILE),
    )

    def block_costs(tile_x, norm_x, tiles_y, norms_y):
        products = jnp.einsum("gie,gbje->gbij", tile_x, tiles_y, preferred_element_type=jnp.float32)
        return norm_x[:, None, :, None] + norms_y[:, :, None, :] - products

    def row_update(potential_g):
        grid_g = potential_g.reshape(target_count, TILE)

        def row_block(carry, items):
            tile_x, norm_x, indices, usable, tiles_y, norms_y = items
            costs = block_costs(tile_x, norm_x, tiles_y, norms_y)
            scores = (grid_g[indices][:, :, None, :] - costs) / epsilon
            scores = jnp.where(usable[:, :, None, None], scores, lowest)
            peak = jnp.max(scores, axis=(1, 3))
            total = jnp.sum(jnp.exp(scores - peak[:, None, :, None]), axis=(1, 3))
            return (carry, (peak, total))

        _, (peaks, totals) = lax.scan(row_block, None, scanned)
        peaks, totals = joined((peaks.reshape(-1), totals.reshape(-1)), "tgt", combine_stats)
        return epsilon * log_source - epsilon * (peaks + jnp.log(totals))

    def column_scores(tile_x, norm_x, tiles_y, norms_y, row_f):
        costs = block_costs(tile_x, norm_x, tiles_y, norms_y)
        return (row_f[:, None, :, None] - costs) / epsilon

    def column_update(potential_f):
        grid_f = potential_f.reshape(blocks, group, TILE)
        inputs = scanned + (grid_f,)

        def highest_step(highest, items):
            tile_x, norm_x, indices, usable, tiles_y, norms_y, row_f = items
            scores = column_scores(tile_x, norm_x, tiles_y, norms_y, row_f)
            block_peak = jnp.where(usable[:, :, None], jnp.max(scores, axis=2), lowest)
            return (highest.at[indices].max(block_peak), None)

        highest, _ = lax.scan(
            highest_step, jnp.full((target_count, TILE), lowest, jnp.float32), inputs
        )
        highest = lax.pmax(highest, "src")

        def mass_step(masses, items):
            tile_x, norm_x, indices, usable, tiles_y, norms_y, row_f = items
            scores = column_scores(tile_x, norm_x, tiles_y, norms_y, row_f)
            block_mass = jnp.sum(jnp.exp(scores - highest[indices][:, :, None, :]), axis=2)
            block_mass = jnp.where(usable[:, :, None], block_mass, 0.0)
            return (masses.at[indices].add(block_mass), None)

        masses, _ = lax.scan(mass_step, jnp.zeros((target_count, TILE), jnp.float32), inputs)
        masses = lax.psum(masses, "src")
        return (epsilon * log_target - epsilon * (highest + jnp.log(masses))).reshape(-1)

    potential_g = jnp.zeros((target_points.shape[0],), jnp.float32)
    potential_f = jnp.zeros((source_points.shape[0],), jnp.float32)
    for iteration in range(ITERS):
        potential_f = row_update(potential_g)
        potential_g = column_update(potential_f)
    return (potential_f, potential_g)


def solution(mesh):
    in_specs = (P("src", None), P("tgt", None), P("src", "tgt", None), P("src", "tgt"))
    out_specs = (P("src"), P("tgt"))
    return jax.shard_map(local, mesh=mesh, in_specs=in_specs, out_specs=out_specs, check_vma=False)
```

profile of v0, /device:TPU:2, one launch (start us, length us, event | category | flops | bytes accessed | tf_op | source)
XLA Modules:
  0.0 1392.0 jit_solution(1863528109426024308)
XLA Ops:
  10.8 3.2 multiply_reduce_fusion
  14.0 4.8 copy.224
  18.8 2.9 gather_fusion.9
  22.9 14.5 %while.176 = (s32[]{:T(128)}, f32[2,8,256]{2,1,0:T(8,128)S(1)}, f32[2,8,256]{2,1,0:T(8,128)S(1)}, pred[2,8,4]{1,2,0:T(4,128)(4,1)S(1)}, s32[2,8,4]{1,2,0:T(4,128...) while((s32[]{:T(128)}, f32[2,8,256]{2,1,0:T(8,128)S(1)}, ...), condition=%wide.region_5.6_spmd, body=%wide.region_2.5_spmd.sunk | while | flops 291501152 | bytes 18644260 | solution.py:71
  23.9 3.6 fusion.137
  27.4 2.7 exponential_reduce_fusion.8
  31.1 3.6 fusion.137
  34.7 2.7 exponential_reduce_fusion.8
  37.4 12.8 all-gather
  50.3 12.8 all-gather.1
  63.9 6.1 while.178
  63.9 1.8 fusion.140
  67.0 1.8 fusion.140
  70.7 143.7 %all-reduce.9.cloned.1.call-done = f32[128,256]{1,0:T(8,128)} async-done(((f32[128,256]{1,0:T(8,128)}), f32[128,256]{1,0:T(8,128)}) %all-reduce.9.cloned.1.call-update) | async-done | bytes 131088 | tf_op jit(solution)/shard_map/pmax | solution.py:92
  214.5 11.2 while.179
  216.3 2.7 fusion.143
  220.3 1.5 gather_fusion.1
  221.8 2.7 fusion.143
  226.4 139.3 %all-reduce.11.cloned.1.call-done = f32[128,256]{1,0:T(8,128)} async-done(((f32[128,256]{1,0:T(8,128)}), f32[128,256]{1,0:T(8,128)}) %all-reduce.11.cloned.1.call-update) | async-done | bytes 131088 | tf_op jit(solution)/shard_map/psum | solution.py:102
  366.7 14.5 %while.180 = (s32[]{:T(128)}, f32[2,8,256]{2,1,0:T(8,128)S(1)}, f32[2,8,256]{2,1,0:T(8,128)S(1)}, pred[2,8,4]{1,2,0:T(4,128)(4,1)S(1)}, s32[2,8,4]{1,2,0:T(4,128...) while((s32[]{:T(128)}, f32[2,8,256]{2,1,0:T(8,128)S(1)}, ...), condition=%wide.region_21.22_spmd, body=%wide.region_18.21_spmd.sunk | while | flops 291501152 | bytes 18513184 | solution.py:71
  367.6 3.6 fusion.145
  371.2 2.7 exponential_reduce_fusion.9
  374.9 3.6 fusion.145
  378.5 2.7 exponential_reduce_fusion.9
  381.2 12.8 all-gather.2
  394.0 12.9 all-gather.3
  407.8 6.1 while.182
  407.8 1.8 fusion.148
  410.9 1.8 fusion.148
  414.6 139.0 %all-reduce.13.cloned.1.call-done = f32[128,256]{1,0:T(8,128)} async-done(((f32[128,256]{1,0:T(8,128)}), f32[128,256]{1,0:T(8,128)}) %all-reduce.13.cloned.1.call-update) | async-done | bytes 131088 | tf_op jit(solution)/shard_map/pmax | solution.py:92
  553.6 11.2 while.183
  555.4 2.7 fusion.151
  561.0 2.7 fusion.151
  565.5 139.3 %all-reduce.15.cloned.1.call-done = f32[128,256]{1,0:T(8,128)} async-done(((f32[128,256]{1,0:T(8,128)}), f32[128,256]{1,0:T(8,128)}) %all-reduce.15.cloned.1.call-update) | async-done | bytes 131088 | tf_op jit(solution)/shard_map/psum | solution.py:102
  705.8 14.5 %while.184 = (s32[]{:T(128)}, f32[2,8,256]{2,1,0:T(8,128)S(1)}, f32[2,8,256]{2,1,0:T(8,128)S(1)}, pred[2,8,4]{1,2,0:T(4,128)(4,1)S(1)}, s32[2,8,4]{1,2,0:T(4,128...) while((s32[]{:T(128)}, f32[2,8,256]{2,1,0:T(8,128)S(1)}, ...), condition=%wide.region_37.38_spmd, body=%wide.region_34.37_spmd.sunk | while | flops 291501152 | bytes 18513184 | solution.py:71
  706.8 3.6 fusion.153
  710.4 2.7 exponential_reduce_fusion.10
  714.1 3.6 fusion.153
  717.7 2.7 exponential_reduce_fusion.10
  720.4 12.8 all-gather.4
  733.2 12.8 all-gather.5
  746.8 6.1 while.186
  746.8 1.8 fusion.156
  749.9 1.8 fusion.156
  753.6 139.0 %all-reduce.17.cloned.1.call-done = f32[128,256]{1,0:T(8,128)} async-done(((f32[128,256]{1,0:T(8,128)}), f32[128,256]{1,0:T(8,128)}) %all-reduce.17.cloned.1.call-update) | async-done | bytes 131088 | tf_op jit(solution)/shard_map/pmax | solution.py:92
  892.6 11.2 while.187
  894.4 2.7 fusion.159
  899.9 2.7 fusion.159
  904.5 139.2 %all-reduce.19.cloned.1.call-done = f32[128,256]{1,0:T(8,128)} async-done(((f32[128,256]{1,0:T(8,128)}), f32[128,256]{1,0:T(8,128)}) %all-reduce.19.cloned.1.call-update) | async-done | bytes 131088 | tf_op jit(solution)/shard_map/psum | solution.py:102
  1044.7 14.5 %while.188 = (s32[]{:T(128)}, f32[2,8,256]{2,1,0:T(8,128)S(1)}, f32[2,8,256]{2,1,0:T(8,128)S(1)}, pred[2,8,4]{1,2,0:T(4,128)(4,1)S(1)}, s32[2,8,4]{1,2,0:T(4,128...) while((s32[]{:T(128)}, f32[2,8,256]{2,1,0:T(8,128)S(1)}, ...), condition=%wide.region_53.54_spmd, body=%wide.region_50.53_spmd.sunk | while | flops 291501152 | bytes 18513184 | solution.py:71
  1045.7 3.6 fusion.161
  1049.3 2.7 exponential_reduce_fusion.11
  1052.9 3.6 fusion.161
  1056.5 2.7 exponential_reduce_fusion.11
  1059.3 12.8 all-gather.6
  1072.1 13.0 all-gather.7
  1086.4 6.1 while.190
  1086.4 1.8 fusion.164
  1089.5 1.8 fusion.164
  1093.3 139.0 %all-reduce.21.cloned.1.call-done = f32[128,256]{1,0:T(8,128)} async-done(((f32[128,256]{1,0:T(8,128)}), f32[128,256]{1,0:T(8,128)}) %all-reduce.21.cloned.1.call-update) | async-done | bytes 131088 | tf_op jit(solution)/shard_map/pmax | solution.py:92
  1232.2 11.2 while.191
  1234.0 2.7 fusion.167
  1239.6 2.7 fusion.167
  1244.1 139.3 %all-reduce.23.cloned.1.call-done = f32[128,256]{1,0:T(8,128)} async-done(((f32[128,256]{1,0:T(8,128)}), f32[128,256]{1,0:T(8,128)}) %all-reduce.23.cloned.1.call-update) | async-done | bytes 131088 | tf_op jit(solution)/shard_map/psum | solution.py:102
  (449 shorter events, 58.7 us)
Async XLA Ops:
  7.2 207.3 %all-reduce.9.cloned.1.call-start = ((), (), s32[]{:S(2)}) async-start(), calls=%async_computation | async-start | bytes 262144 | tf_op jit(solution)/shard_map/pmax | solution.py:92
  14.0 8.4 copy-start.8
  70.0 0.7 copy-start.2
  70.7 295.0 %all-reduce.11.cloned.1.call-start = ((), (), s32[]{:S(2)}) async-start(), calls=%async_computation.1 | async-start | bytes 262144 | tf_op jit(solution)/shard_map/psum | solution.py:102
  225.7 0.7 copy-start.3
  226.3 327.3 %all-reduce.13.cloned.1.call-start = ((), (), s32[]{:S(2)}) async-start(), calls=%async_computation.2 | async-start | bytes 262144 | tf_op jit(solution)/shard_map/pmax | solution.py:92
  413.9 0.7 copy-start.4
  414.6 290.2 %all-reduce.15.cloned.1.call-start = ((), (), s32[]{:S(2)}) async-start(), calls=%async_computation.3 | async-start | bytes 262144 | tf_op jit(solution)/shard_map/psum | solution.py:102
  564.8 0.7 copy-start.5
  565.5 327.1 %all-reduce.17.cloned.1.call-start = ((), (), s32[]{:S(2)}) async-start(), calls=%async_computation.4 | async-start | bytes 262144 | tf_op jit(solution)/shard_map/pmax | solution.py:92
  752.9 0.7 copy-start.6
  753.6 290.1 %all-reduce.19.cloned.1.call-start = ((), (), s32[]{:S(2)}) async-start(), calls=%async_computation.5 | async-start | bytes 262144 | tf_op jit(solution)/shard_map/psum | solution.py:102
  903.8 0.7 copy-start.7
  904.4 327.8 %all-reduce.21.cloned.1.call-start = ((), (), s32[]{:S(2)}) async-start(), calls=%async_computation.6 | async-start | bytes 262144 | tf_op jit(solution)/shard_map/pmax | solution.py:92
  1085.8 0.6 copy-start.9
  1092.5 0.7 copy-start
  1093.2 290.2 %all-reduce.23.cloned.1.call-start = ((), (), s32[]{:S(2)}) async-start(), calls=%async_computation.7 | async-start | bytes 262144 | tf_op jit(solution)/shard_map/psum | solution.py:102
  1243.4 0.7 copy-start.1
Sparse Core Ops, SparseCore 0:
  70.8 143.6 all-reduce.8
  226.5 139.1 all-reduce.10
  414.7 138.8 all-reduce.12
  565.6 139.1 all-reduce.14
  753.7 138.8 all-reduce.16
  904.6 139.0 all-reduce.18
  1093.3 138.8 all-reduce.20
  1244.2 139.1 all-reduce.22
where the time goes:
time: 1390 us
  waiting for transfers between devices  1120 us (81%)
  blocking collectives  102 us (7%)
  matrix products  64.5 us (5%)
  other arithmetic  46.5 us (3%)
  local copies, waits for them, and re-layouts  43 us (3%)
  between operations  14.8 us (1%)
    pmax x4, waiting for transfers between devices, column_update(): highest = lax.pmax(highest, 'src')  561 us
    psum x4, waiting for transfers between devices, column_update(): masses = lax.psum(masses, 'src')  557 us
    all_gather x8, blocking collectives, joined(): pieces = jax.tree.map(lambda part: lax.all_gather(part, axis), value)  102 us
    dot_general x24, matrix products, block_costs(): jnp.einsum('gie,gbje->gbij', tile_x, tiles_y, preferred_element_type=jnp....  64.5 us
  transfers between devices with their start and end apart: 8, of which 8 were waited for; matrix products, arithmetic and copies ran while one was open for 0% of the time, Pallas kernels for 0%

commit v1 on v0

v1 whole, which is shorter than its diff:
```python
import functools
import math

import jax
import jax.numpy as jnp
from jax import lax
from jax.experimental import pallas as pl
from jax.experimental.pallas import tpu as pltpu
from jax.sharding import PartitionSpec as P

TILE = 256
HALF = 128
E = 64
KLOC = 4
ITERS = 4
LOWEST = -1e30
SHIFT = 32.0
LOG2E = math.log2(math.e)
LN2 = math.log(2.0)
CHUNK = 128
UNROLL = 4
LANES = (slice(0, HALF), slice(HALF, TILE))
VMEM_LIMIT = 12 * 1024 * 1024
RESIDENT = True


def held(x, space):
    return pltpu.with_memory_space_constraint(x, space) if RESIDENT else x


def like(shape, dtype=jnp.float32):
    return pltpu.VMEM(shape, dtype) if RESIDENT else jax.ShapeDtypeStruct(shape, dtype)


SPACE = {"s": pltpu.SMEM, "v": pltpu.VMEM, "k": pltpu.VMEM, "w": pltpu.VMEM, "a": pl.ANY, "h": pltpu.HBM}


def call(kernel, outs, out_specs, specs, args, scratch=(), name=None):
    specs_of = lambda letters: [pl.BlockSpec(memory_space=SPACE[s]) for s in letters]
    args = [held(arg, SPACE[spec]) if spec in "vkwh" else arg for spec, arg in zip(specs, args, strict=True)]
    keep = max(specs.find("k"), specs.find("w"))
    if keep >= 0:
        outs, out_specs = (*outs, like(args[keep].shape, args[keep].dtype)), out_specs + ("a" if "k" in specs else "v")
    return pl.pallas_call(
        kernel,
        out_shape=tuple(outs),
        in_specs=specs_of(specs),
        out_specs=tuple(specs_of(out_specs)),
        scratch_shapes=list(scratch),
        input_output_aliases={keep: len(outs) - 1} if keep >= 0 else {},
        compiler_params=pltpu.CompilerParams(vmem_limit_bytes=VMEM_LIMIT),
        name=name,
    )(*args)


class Codes:
    def __init__(self, held, codes, sem):
        self.copy = pltpu.make_async_copy(held, codes, sem.at[0])
        self.copy.start()
        self.codes = codes

    def ready(self):
        self.copy.wait()
        return self.codes


def for_blocks(codes, tiles, block):
    count = codes[codes.shape[0] - 1]

    def one(i):
        slot = lax.div(codes[i], tiles)
        block(slot, lax.div(slot, KLOC), codes[i] - slot * tiles)

    def several(i, _):
        for j in range(UNROLL):
            one(i * UNROLL + j)
        return 0

    def single(i, _):
        one(i)
        return 0

    groups = lax.div(count, UNROLL)
    lax.fori_loop(0, groups, several, 0)
    lax.fori_loop(groups * UNROLL, count, single, 0)


def place(t):
    return pl.ds(pl.multiple_of(t * TILE, TILE), TILE)


def spread_tiles(rows, tall):
    for p in range(tall.shape[0]):
        for h in range(2):
            row = rows[2 * p + h : 2 * p + h + 1, :]
            tall[p, LANES[h], :] = jnp.broadcast_to(row, (HALF, HALF)).T


def lane_join(tall, join):
    rows = []
    for p in range(tall.shape[0]):
        for h in range(2):
            rows.append(join(tall[p, LANES[h], :].T, axis=0, keepdims=True))
    return jnp.concatenate(rows, axis=0)


def fill(out, value):
    for d in range(out.shape[0]):
        out[d] = value


def total_of(parts):
    return functools.reduce(jnp.add, parts)


def parts_of(ref):
    return [ref[d] for d in range(ref.shape[0])]


def lse_of(parts):
    top = functools.reduce(jnp.maximum, parts)
    return top + jnp.log2(total_of([jnp.exp2(part - top) for part in parts]))


def product(a, b):
    return jnp.dot(a, b, preferred_element_type=jnp.float32)


def half_norms(points):
    wide = points.astype(jnp.float32)
    return 0.5 * jnp.sum(wide * wide, axis=0, keepdims=True)


def lane_rows(row):
    return jnp.concatenate([row[:, i : i + HALF] for i in range(0, row.shape[1], HALF)], axis=0)


def row_first_kernel(
    lists_in, counts_in, me, x, y, codes, out, inner, x_norms, share_norms, tx, ty, lists, counts, xs, top, mass, sems
):
    tiles, targets = xs.shape[0], ty.shape[1] // TILE
    pairs = ((lists_in, lists), (counts_in, counts), (x, tx), (y, ty))
    copies = [pltpu.make_async_copy(*pair, sems.at[i]) for i, pair in enumerate(pairs)]
    for copy in copies:
        copy.start()
    copies[0].wait()
    copies[1].wait()

    def listed(p, n):
        for k in range(KLOC):
            codes[n + k] = (p * KLOC + k) * targets + lists[k, p]
        return n + counts[p]

    codes[codes.shape[0] - 1] = lax.fori_loop(0, tiles, listed, 0)
    top[...] = jnp.full_like(top, LOWEST)
    mass[...] = jnp.zeros_like(mass)
    copies[2].wait()
    norms = []
    for p in range(tiles):
        points = tx[:, p * TILE : (p + 1) * TILE]
        norms.append(lane_rows(half_norms(points)))
        xs[p] = points.astype(jnp.float32).T.astype(jnp.bfloat16)
    x_norms[...] = jnp.concatenate(norms, axis=0)
    copies[3].wait()
    width = share_norms.shape[0] * HALF
    share_norms[...] = lane_rows(half_norms(ty[:, pl.ds(pl.multiple_of(me[0] * width, width), width)]))

    def block(slot, p, t):
        points = ty[:, place(t)]
        norms = half_norms(points) * LOG2E
        for r in range(0, TILE, CHUNK):
            rows = slice(r, r + CHUNK)
            scores = product(xs[p, rows, :], points) * LOG2E
            inner[slot, rows, :] = scores
            scores -= norms
            one, two = scores[:, LANES[0]], scores[:, LANES[1]]
            old = top[p, rows, :]
            new = jnp.maximum(old, jnp.maximum(one, two))
            top[p, rows, :] = new
            mass[p, rows, :] = mass[p, rows, :] * jnp.exp2(old - new) + (jnp.exp2(one - new) + jnp.exp2(two - new))

    for_blocks(codes, targets, block)
    lses = []
    for p in range(tiles):
        for h in range(2):
            tops, masses = top[p, LANES[h], :].T, mass[p, LANES[h], :].T
            peak = jnp.max(tops, axis=0, keepdims=True)
            lses.append(peak + jnp.log2(jnp.sum(masses * jnp.exp2(tops - peak), axis=0, keepdims=True)))
    fill(out, jnp.concatenate(lses, axis=0))


def both(tall):
    return jnp.concatenate([tall, tall], axis=1)


def col_first_kernel(log_ns, held_codes, inner, parts, u, out, _, peak, total, tall, codes, sem):
    blocks = Codes(held_codes, codes, sem)
    rows = -log_ns - lse_of(parts_of(parts))
    u[...] = rows
    peak[...] = jnp.full_like(peak, LOWEST)
    total[...] = jnp.zeros_like(total)
    spread_tiles(rows, tall)

    def block(slot, p, t):
        scores = inner[slot] + both(tall[p])
        old = peak[t]
        new = jnp.maximum(old, jnp.max(scores, axis=0, keepdims=True))
        mass = jnp.sum(jnp.exp2(scores - new), axis=0, keepdims=True)
        peak[t] = new
        total[t] = total[t] * jnp.exp2(old - new) + mass

    for_blocks(blocks.ready(), out.shape[0], block)
    masses = total[...]
    out[...] = jnp.where(masses > 0.0, peak[...] + jnp.log2(masses), LOWEST)


def plan_kernel(held_codes, inner, u, w, out, plan, tall, acc, codes, sem):
    blocks = Codes(held_codes, codes, sem)
    spread_tiles(u[...] + SHIFT, tall)
    acc[...] = jnp.zeros_like(acc)

    def block(slot, p, t):
        column = w[t]
        for r in range(0, TILE, CHUNK):
            rows = slice(r, r + CHUNK)
            part = jnp.exp2(inner[slot, rows, :] + both(tall[p, rows, :]) + column)
            plan[slot, rows, :] = part
            acc[p, rows, :] += part[:, LANES[0]] + part[:, LANES[1]]

    for_blocks(blocks.ready(), w.shape[0], block)
    fill(out, lane_join(acc, jnp.sum))


def row_kernel(held_codes, plan, b, out, _, acc, codes, sem):
    blocks = Codes(held_codes, codes, sem)
    acc[...] = jnp.zeros_like(acc)

    def block(slot, p, t):
        first, second = b[t, :, LANES[0]], b[t, :, LANES[1]]
        for r in range(0, TILE, CHUNK):
            rows = slice(r, r + CHUNK)
            acc[p, rows, :] += plan[slot, rows, LANES[0]] * first + plan[slot, rows, LANES[1]] * second

    for_blocks(blocks.ready(), b.shape[0], block)
    fill(out, lane_join(acc, jnp.sum))


def col_kernel(ns, last, held_codes, plan, parts, *refs):
    u, x_norms, out, f, _, acc, tall, codes, sem = refs if last else (None, None, refs[0], None, *refs[1:])
    blocks = Codes(held_codes, codes, sem)
    a = 1.0 / (ns * total_of(parts_of(parts)))
    spread_tiles(a, tall)
    if last:
        f[...] = (u[...] + (jnp.log2(a) + SHIFT)) * LN2 + x_norms[...]
    acc[...] = jnp.zeros_like(acc)

    def block(slot, p, t):
        sums = [[None] * 2, [None] * 2]
        for r in range(0, TILE, 8):
            factor = tall[p, r : r + 8, :]
            for h in range(2):
                term = plan[slot, r : r + 8, LANES[h]] * factor
                chain = (r // 8) % 2
                sums[h][chain] = term if sums[h][chain] is None else sums[h][chain] + term
        for h in range(2):
            acc[t, :, LANES[h]] += sums[h][0] + sums[h][1]

    for_blocks(blocks.ready(), out.shape[0], block)
    out[...] = jnp.sum(acc[...], axis=1, keepdims=True)


def join_first_kernel(log_nt, parts, w, out):
    w[...] = -log_nt - lse_of(parts_of(parts))
    fill(out, w[...])


def join_kernel(nt, parts, out):
    fill(out, 1.0 / (nt * total_of(parts_of(parts))))


def join_last_kernel(log_nt, parts, w, share_norms, out):
    fill(out, (w[...] + (-log_nt - jnp.log2(total_of(parts_of(parts))))) * LN2 + share_norms[...])


def trade_tgt(pieces):
    return lax.all_to_all(pieces, "tgt", 0, 0)


def trade_src(pieces):
    return lax.all_to_all(pieces, "src", 0, 0)


def iterate(x, y, lists, counts, me, ns, nt, n_src, n_tgt, trade_tgt, trade_src):
    st, tt = x.shape[0] // TILE, y.shape[0] // TILE
    shape = (2 * st, HALF)
    share = (2 * tt // n_src, HALF)
    plain = lambda *shape: jax.ShapeDtypeStruct(shape, jnp.float32)
    scratch = lambda *shape: pltpu.VMEM(shape, jnp.float32)
    row, rows, col, cell, cells = like(shape), like((n_tgt, *shape)), like((tt, 1, TILE)), like(share), like((n_src, *share))
    length = (st * KLOC // HALF + 1) * HALF
    codes = jax.ShapeDtypeStruct((length,), jnp.int32)
    fetch = (pltpu.SMEM((length,), jnp.int32), pltpu.SemaphoreType.DMA((1,)))
    tall, stats = scratch(st, TILE, HALF), scratch(tt, 1, TILE)
    log_ns, log_nt = math.log2(ns), math.log2(nt)
    pieces = lambda v: trade_src(v.reshape((n_src, *share)))
    whole = lambda v: trade_src(v).reshape(tt, 1, TILE)

    blocks = like((st * KLOC, TILE, TILE))
    codes, lse, inner, x_norms, share_norms = call(
        row_first_kernel,
        (codes, rows, blocks, row, cell),
        "svvvv",
        "hhshh",
        (lists.T, counts, me, x.T, y.T),
        (
            pltpu.VMEM((E, st * TILE), jnp.bfloat16),
            pltpu.VMEM((E, tt * TILE), jnp.bfloat16),
            pltpu.SMEM((KLOC, st), jnp.int32),
            pltpu.SMEM((st,), jnp.int32),
            pltpu.VMEM((st, TILE, E), jnp.bfloat16),
            tall,
            tall,
            pltpu.SemaphoreType.DMA((4,)),
        ),
        "row_first",
    )
    u, lse, inner = call(
        functools.partial(col_first_kernel, log_ns), (row, col), "vv", "vkv", (codes, inner, trade_tgt(lse)),
        (stats, stats, tall, *fetch), "col_first",
    )
    w, share_w = call(functools.partial(join_first_kernel, log_nt), (cell, cells), "vv", "v", (pieces(lse),), (), "join")
    mass, plan = call(plan_kernel, (rows,), "v", "vwvv", (codes, inner, u, whole(share_w)), (tall, tall, *fetch), "plan")
    for iteration in range(1, ITERS):
        last = iteration == ITERS - 1
        mass, *f, plan = call(
            functools.partial(col_kernel, ns, last), (col, plain(*shape)) if last else (col,), "vv" if last else "v",
            "vkvvv" if last else "vkv", (codes, plan, trade_tgt(mass)) + ((u, x_norms) if last else ()),
            (scratch(tt, 8, TILE), tall, *fetch), "col",
        )
        if last:
            break
        (b,) = call(functools.partial(join_kernel, nt), (cells,), "v", "v", (pieces(mass),), (), "join")
        mass, plan = call(row_kernel, (rows,), "v", "vkv", (codes, plan, whole(b)), (tall, *fetch), "row")
    (g,) = call(
        functools.partial(join_last_kernel, log_nt), (cells,), "v", "vvv", (pieces(mass), w, share_norms), (), "join"
    )
    return f[0].reshape(-1), trade_src(g).reshape(-1)


def local(source_points, target_points, tile_lists, tile_counts):
    n_src, n_tgt = lax.axis_size("src"), lax.axis_size("tgt")
    ns, nt = source_points.shape[0] * n_src, target_points.shape[0] * n_tgt
    me = lax.axis_index("src").astype(jnp.int32).reshape(1)
    return iterate(
        source_points, target_points, tile_lists[:, 0, :], tile_counts[:, 0], me, ns, nt, n_src, n_tgt, trade_tgt, trade_src
    )


def solution(mesh):
    in_specs = (P("src", None), P("tgt", None), P("src", "tgt", None), P("src", "tgt"))
    out_specs = (P("src"), P("tgt"))
    return jax.shard_map(local, mesh=mesh, in_specs=in_specs, out_specs=out_specs, check_vma=False)
```

time: 1390 us -> 182 us (0.13)
  waiting for transfers between devices: 1120 us -> 0 us
  matrix products: 64.5 us -> 0 us
  blocking collectives: 102 us -> 155 us
  other arithmetic: 46.5 us -> 0 us
  local copies, waits for them, and re-layouts: 43 us -> 0.66 us
  Pallas kernels: 0 us -> 25 us
  between operations: 14.8 us -> 0.72 us
    pmax x4 -> x0, waiting for transfers between devices: 561 us -> none  [column_update(): highest = lax.pmax(highest, 'src')]
    psum x4 -> x0, waiting for transfers between devices: 557 us -> none  [column_update(): masses = lax.psum(masses, 'src')]
    all_to_all x0 -> x12, blocking collectives: none -> 155 us  [the longest x8 117 us: trade_src(): return lax.all_to_all(pieces, 'src', 0, 0)]
    all_gather x8 -> x0, blocking collectives: 102 us -> none  [joined(): pieces = jax.tree.map(lambda part: lax.all_gather(part, axis), value)]
    dot_general x24 -> x0, matrix products: 64.5 us -> none  [block_costs(): jnp.einsum('gie,gbje->gbij', tile_x, tiles_y, preferred_element_type=jnp....]
    pallas_call x0 -> x12, Pallas kernels: none -> 25 us  [call(): pl.pallas_call(kernel, out_shape=tuple(outs), in_specs=specs_of(specs), o...]
    reduce_sum x10 -> x0, other arithmetic: 24.7 us -> none  [the longest x8 21.3 us: row_block(): total = jnp.sum(jnp.exp(scores - peak[:, None, :, None]), axis=(1, 3))]
    gather x34 -> x0, local copies, waits for them, and re-layouts: 20.6 us -> none  [the longest x16 12.2 us: mass_step(): highest[indices][:, :, None, :]]
  transfers between devices with their start and end apart: 8 -> 0, of which waited for: 8 -> 0; matrix products, arithmetic and copies ran while one was open for 0% -> 0% of each run, Pallas kernels for 0% -> 0%
where the time goes in v1:
time: 182 us; the launch traced here: 181 us
  blocking collectives  155 us (85%)
  Pallas kernels  25 us (14%)
    all_to_all x8, blocking collectives, trade_src(): return lax.all_to_all(pieces, 'src', 0, 0)  117 us
    all_to_all x4, blocking collectives, trade_tgt(): return lax.all_to_all(pieces, 'tgt', 0, 0)  37.5 us
    pallas_call x12, Pallas kernels, call(): pl.pallas_call(kernel, out_shape=tuple(outs), in_specs=specs_of(specs), o...  25 us

profile of v1, /device:TPU:2, one launch (start us, length us, event | category | flops | bytes accessed | tf_op | source)
XLA Modules:
  0.0 181.2 jit_solution(16319058813908129081)
XLA Ops:
  0.6 7.6 %row_first.1 = (s32[128]{0:T(128)S(1)}, f32[8,32,128]{2,1,0:T(8,128)S(1)}, f32[64,256,256]{2,1,0:T(8,128)S(1)}, f32[32,128]{1,0:T(8,128)S(1)}, f32[8,128]{1,0:T(8,128)S(1)}) custom-call(s32[4,16]{1,0:T(4,128)} %bitcast.26, s32[16]{0:T(128)} %bitcast.27, s32[1]{0:T(128)} %bitcast.3.me, bf16[64,4096]{1,0:T(8,128)(2,1)} %bitcast.24, bf16[64,32768]{1,0:T(8,128)(2,1)} %bitcast.23), custom_call_target="tpu_custom_call" | custom-call | tf_op jit(solution)/shard_map/row_first/pallas_call | solution.py:44
  8.3 10.6 %all_to_all.60.parts = f32[8,32,128]{2,1,0:T(8,128)S(1)} all-to-all(f32[8,32,128]{2,1,0:T(8,128)S(1)} %get-tuple-element.26), channel_id=1, replica_groups=mesh['src'=32,'tgt'=8] {'tgt'}, dimensions={0} | all-to-all | bytes 262144 | tf_op jit(solution)/shard_map/all_to_all | solution.py:286
  18.9 3.4 %col_first.1 = (f32[32,128]{1,0:T(8,128)S(1)}, f32[128,1,256]{2,1,0:T(1,128)S(1)}, f32[64,256,256]{2,1,0:T(8,128)S(1)}) custom-call(s32[128]{0:T(128)S(1)} %get-tuple-element.24.held_codes, f32[64,256,256]{2,1,0:T(8,128)S(1)} %get-tuple-element.25.inner, f32[8,32,128]{2,1,0:T(8,128)S(1)} %all_to_all.60.parts), custom_call_target="tpu_custom_call", output_to_operand_aliasing={{2}: (1, {})} | custom-call | tf_op jit(solution)/shard_map/col_first/pallas_call | solution.py:44
  22.4 20.5 %all_to_all.61.parts = f32[32,8,128]{2,1,0:T(8,128)S(1)} all-to-all(f32[32,8,128]{2,1,0:T(8,128)S(1)} %bitcast.20), channel_id=1, replica_groups=mesh['src'=32,'tgt'=8] {'src'}, dimensions={0} | all-to-all | bytes 262144 | tf_op jit(solution)/shard_map/all_to_all | solution.py:290
  42.9 0.1 join.4
  43.0 14.0 %all_to_all.62 = f32[32,8,128]{2,1,0:T(8,128)S(1)} all-to-all(f32[32,8,128]{2,1,0:T(8,128)S(1)} %get-tuple-element.30), channel_id=1, replica_groups=mesh['src'=32,'tgt'=8] {'src'}, dimensions={0} | all-to-all | bytes 262144 | tf_op jit(solution)/shard_map/all_to_all | solution.py:290
  56.9 3.4 %plan.1 = (f32[8,32,128]{2,1,0:T(8,128)S(1)}, f32[64,256,256]{2,1,0:T(8,128)S(1)}) custom-call(s32[128]{0:T(128)S(1)} %get-tuple-element.24.held_codes, f32[64,256,256]{2,1,0:T(8,128)S(1)} %get-tuple-element.27.inner, f32[32,128]{1,0:T(8,128)S(1)} %get-tuple-element.28.u.refs_0_, f32[128,1,256]{2,1,0:T(1,128)S(1)} %bitcast.16), custom_call_target="tpu_custom_call", output_to_operand_aliasing={{1}: (1, {})} | custom-call | tf_op jit(solution)/shard_map/plan/pallas_call | solution.py:44
  60.3 9.5 %all_to_all.63.parts = f32[8,32,128]{2,1,0:T(8,128)S(1)} all-to-all(f32[8,32,128]{2,1,0:T(8,128)S(1)} %get-tuple-element.32), channel_id=1, replica_groups=mesh['src'=32,'tgt'=8] {'tgt'}, dimensions={0} | all-to-all | bytes 262144 | tf_op jit(solution)/shard_map/all_to_all | solution.py:286
  69.8 1.9 %col.3 = (f32[128,1,256]{2,1,0:T(1,128)S(1)}, f32[64,256,256]{2,1,0:T(8,128)S(1)}) custom-call(s32[128]{0:T(128)S(1)} %get-tuple-element.24.held_codes, f32[64,256,256]{2,1,0:T(8,128)S(1)} %get-tuple-element.31.plan, f32[8,32,128]{2,1,0:T(8,128)S(1)} %all_to_all.63.parts), custom_call_target="tpu_custom_call", output_to_operand_aliasing={{1}: (1, {})} | custom-call | tf_op jit(solution)/shard_map/col/pallas_call | solution.py:44
  71.7 13.6 %all_to_all.64.parts = f32[32,8,128]{2,1,0:T(8,128)S(1)} all-to-all(f32[32,8,128]{2,1,0:T(8,128)S(1)} %bitcast.21), channel_id=1, replica_groups=mesh['src'=32,'tgt'=8] {'src'}, dimensions={0} | all-to-all | bytes 262144 | tf_op jit(solution)/shard_map/all_to_all | solution.py:290
  85.4 13.9 %all_to_all.65 = f32[32,8,128]{2,1,0:T(8,128)S(1)} all-to-all(f32[32,8,128]{2,1,0:T(8,128)S(1)} %join.5), channel_id=1, replica_groups=mesh['src'=32,'tgt'=8] {'src'}, dimensions={0} | all-to-all | bytes 262144 | tf_op jit(solution)/shard_map/all_to_all | solution.py:290
  99.3 2.1 %row.2 = (f32[8,32,128]{2,1,0:T(8,128)S(1)}, f32[64,256,256]{2,1,0:T(8,128)S(1)}) custom-call(s32[128]{0:T(128)S(1)} %get-tuple-element.24.held_codes, f32[64,256,256]{2,1,0:T(8,128)S(1)} %get-tuple-element.33.plan, f32[128,1,256]{2,1,0:T(1,128)S(1)} %bitcast.17), custom_call_target="tpu_custom_call", output_to_operand_aliasing={{1}: (1, {})} | custom-call | tf_op jit(solution)/shard_map/row/pallas_call | solution.py:44
  101.4 8.7 %all_to_all.66.parts = f32[8,32,128]{2,1,0:T(8,128)S(1)} all-to-all(f32[8,32,128]{2,1,0:T(8,128)S(1)} %get-tuple-element.36), channel_id=1, replica_groups=mesh['src'=32,'tgt'=8] {'tgt'}, dimensions={0} | all-to-all | bytes 262144 | tf_op jit(solution)/shard_map/all_to_all | solution.py:286
  110.2 1.9 %col.4 = (f32[128,1,256]{2,1,0:T(1,128)S(1)}, f32[64,256,256]{2,1,0:T(8,128)S(1)}) custom-call(s32[128]{0:T(128)S(1)} %get-tuple-element.24.held_codes, f32[64,256,256]{2,1,0:T(8,128)S(1)} %get-tuple-element.35.plan, f32[8,32,128]{2,1,0:T(8,128)S(1)} %all_to_all.66.parts), custom_call_target="tpu_custom_call", output_to_operand_aliasing={{1}: (1, {})} | custom-call | tf_op jit(solution)/shard_map/col/pallas_call | solution.py:44
  112.0 13.7 %all_to_all.67.parts = f32[32,8,128]{2,1,0:T(8,128)S(1)} all-to-all(f32[32,8,128]{2,1,0:T(8,128)S(1)} %bitcast.22), channel_id=1, replica_groups=mesh['src'=32,'tgt'=8] {'src'}, dimensions={0} | all-to-all | bytes 262144 | tf_op jit(solution)/shard_map/all_to_all | solution.py:290
  125.8 13.9 %all_to_all.68 = f32[32,8,128]{2,1,0:T(8,128)S(1)} all-to-all(f32[32,8,128]{2,1,0:T(8,128)S(1)} %join.6), channel_id=1, replica_groups=mesh['src'=32,'tgt'=8] {'src'}, dimensions={0} | all-to-all | bytes 262144 | tf_op jit(solution)/shard_map/all_to_all | solution.py:290
  139.7 2.1 %row.3 = (f32[8,32,128]{2,1,0:T(8,128)S(1)}, f32[64,256,256]{2,1,0:T(8,128)S(1)}) custom-call(s32[128]{0:T(128)S(1)} %get-tuple-element.24.held_codes, f32[64,256,256]{2,1,0:T(8,128)S(1)} %get-tuple-element.37.plan, f32[128,1,256]{2,1,0:T(1,128)S(1)} %bitcast.18), custom_call_target="tpu_custom_call", output_to_operand_aliasing={{1}: (1, {})} | custom-call | tf_op jit(solution)/shard_map/row/pallas_call | solution.py:44
  141.8 8.7 %all_to_all.69.parts = f32[8,32,128]{2,1,0:T(8,128)S(1)} all-to-all(f32[8,32,128]{2,1,0:T(8,128)S(1)} %get-tuple-element.40), channel_id=1, replica_groups=mesh['src'=32,'tgt'=8] {'tgt'}, dimensions={0} | all-to-all | bytes 262144 | tf_op jit(solution)/shard_map/all_to_all | solution.py:286
  150.5 2.2 %col.5 = (f32[128,1,256]{2,1,0:T(1,128)S(1)}, f32[32,128]{1,0:T(8,128)}, f32[64,256,256]{2,1,0:T(8,128)S(1)}) custom-call(s32[128]{0:T(128)S(1)} %get-tuple-element.24.held_codes, f32[64,256,256]{2,1,0:T(8,128)S(1)} %get-tuple-element.39.plan, f32[8,32,128]{2,1,0:T(8,128)S(1)} %all_to_all.69.parts, ...), custom_call_target="tpu_custom_call", output_to_operand_aliasing={{2}: (1, {})} | custom-call | tf_op jit(solution)/shard_map/col/pallas_call | solution.py:44
  152.8 13.7 %all_to_all.70.parts = f32[32,8,128]{2,1,0:T(8,128)S(1)} all-to-all(f32[32,8,128]{2,1,0:T(8,128)S(1)} %bitcast.19), channel_id=1, replica_groups=mesh['src'=32,'tgt'=8] {'src'}, dimensions={0} | all-to-all | bytes 262144 | tf_op jit(solution)/shard_map/all_to_all | solution.py:290
  166.5 14.0 %all_to_all.71 = f32[32,8,128]{2,1,0:T(8,128)S(1)} all-to-all(f32[32,8,128]{2,1,0:T(8,128)S(1)} %join.7), channel_id=1, replica_groups=mesh['src'=32,'tgt'=8] {'src'}, dimensions={0} | all-to-all | bytes 262144 | tf_op jit(solution)/shard_map/all_to_all | solution.py:290
  180.5 0.7 copy.21
  (3 shorter events, 0.1 us)

commit v2 on v1

v2 whole, which is shorter than its diff:
```python
import functools
import math

import jax
import jax.numpy as jnp
from jax import lax
from jax.experimental import pallas as pl
from jax.experimental.pallas import tpu as pltpu
from jax.sharding import PartitionSpec as P

TILE = 256
HALF = 128
E = 64
KLOC = 4
ITERS = 4
LOWEST = -1e30
SHIFT = 32.0
LOG2E = math.log2(math.e)
LN2 = math.log(2.0)
SMALL = 2.0**-60
CHUNK = 128
LANES = (slice(0, HALF), slice(HALF, TILE))
VMEM_LIMIT = 12 * 1024 * 1024
RESIDENT = True


def held(x, space):
    return pltpu.with_memory_space_constraint(x, space) if RESIDENT else x


def like(shape, dtype=jnp.float32):
    return pltpu.VMEM(shape, dtype) if RESIDENT else jax.ShapeDtypeStruct(shape, dtype)


SPACE = {"s": pltpu.SMEM, "v": pltpu.VMEM, "k": pltpu.VMEM, "w": pltpu.VMEM, "a": pl.ANY, "h": pltpu.HBM}


def call(kernel, outs, out_specs, specs, args, scratch=(), name=None):
    specs_of = lambda letters: [pl.BlockSpec(memory_space=SPACE[s]) for s in letters]
    args = [held(arg, SPACE[spec]) if spec in "vkwh" else arg for spec, arg in zip(specs, args, strict=True)]
    keep = max(specs.find("k"), specs.find("w"))
    if keep >= 0:
        outs, out_specs = (*outs, like(args[keep].shape, args[keep].dtype)), out_specs + ("a" if "k" in specs else "v")
    return pl.pallas_call(
        kernel,
        out_shape=tuple(outs),
        in_specs=specs_of(specs),
        out_specs=tuple(specs_of(out_specs)),
        scratch_shapes=list(scratch),
        input_output_aliases={keep: len(outs) - 1} if keep >= 0 else {},
        compiler_params=pltpu.CompilerParams(vmem_limit_bytes=VMEM_LIMIT),
        name=name,
    )(*args)


class Codes:
    def __init__(self, held, codes, sem):
        self.copy = pltpu.make_async_copy(held, codes, sem.at[0])
        self.copy.start()
        self.codes = codes

    def ready(self):
        self.copy.wait()
        return self.codes


def for_blocks(codes, tiles, block, unroll=4):
    count = codes[codes.shape[0] - 1]

    def one(i):
        slot = lax.div(codes[i], tiles)
        block(slot, lax.div(slot, KLOC), codes[i] - slot * tiles)

    def several(i, _):
        for j in range(unroll):
            one(i * unroll + j)
        return 0

    def single(i, _):
        one(i)
        return 0

    groups = lax.div(count, unroll)
    lax.fori_loop(0, groups, several, 0)
    lax.fori_loop(groups * unroll, count, single, 0)


def place(t):
    return pl.ds(pl.multiple_of(t * TILE, TILE), TILE)


def spread_tiles(rows, tall):
    for p in range(tall.shape[0]):
        for h in range(2):
            row = rows[2 * p + h : 2 * p + h + 1, :]
            tall[p, LANES[h], :] = jnp.broadcast_to(row, (HALF, HALF)).T


def lane_join(tall, join):
    rows = []
    for p in range(tall.shape[0]):
        for h in range(2):
            rows.append(join(tall[p, LANES[h], :].T, axis=0, keepdims=True))
    return jnp.concatenate(rows, axis=0)


def fill(out, value):
    for d in range(out.shape[0]):
        out[d] = value


def total_of(parts):
    return functools.reduce(jnp.add, parts)


def parts_of(ref):
    return [ref[d] for d in range(ref.shape[0])]


def lse_of(parts):
    top = functools.reduce(jnp.maximum, parts)
    return top + jnp.log2(total_of([jnp.exp2(part - top) for part in parts]))


def product(a, b):
    return jnp.dot(a, b, preferred_element_type=jnp.float32)


def half_norms(points):
    wide = points.astype(jnp.float32)
    return 0.5 * jnp.sum(wide * wide, axis=0, keepdims=True)


def lane_rows(row):
    return jnp.concatenate([row[:, i : i + HALF] for i in range(0, row.shape[1], HALF)], axis=0)


def row_first_kernel(lists_in, counts_in, x, y, codes, out, costs, tx, ty, lists, counts, xs, tall, mass, sems):
    tiles, targets = xs.shape[0], ty.shape[1] // TILE
    pairs = ((lists_in, lists), (counts_in, counts), (x, tx), (y, ty))
    copies = [pltpu.make_async_copy(*pair, sems.at[i]) for i, pair in enumerate(pairs)]
    for copy in copies:
        copy.start()
    copies[0].wait()
    copies[1].wait()

    def listed(p, n):
        for k in range(KLOC):
            codes[n + k] = (p * KLOC + k) * targets + lists[k, p]
        return n + counts[p]

    codes[codes.shape[0] - 1] = lax.fori_loop(0, tiles, listed, 0)
    mass[...] = jnp.zeros_like(mass)
    copies[2].wait()
    norms = []
    for p in range(tiles):
        points = tx[:, p * TILE : (p + 1) * TILE]
        norms.append(lane_rows(half_norms(points)))
        xs[p] = points.astype(jnp.float32).T.astype(jnp.bfloat16)
    spread_tiles(jnp.concatenate(norms, axis=0) * LOG2E, tall)
    copies[3].wait()

    def block(slot, p, t):
        points = ty[:, place(t)]
        norms = half_norms(points) * LOG2E
        for r in range(0, TILE, CHUNK):
            rows = slice(r, r + CHUNK)
            scores = (product(xs[p, rows, :], points) * LOG2E - norms) - both(tall[p, rows, :])
            costs[slot, rows, :] = scores
            terms = jnp.exp2(scores)
            mass[p, rows, :] += terms[:, LANES[0]] + terms[:, LANES[1]]

    for_blocks(codes, targets, block, 8)
    sums = lane_join(mass, jnp.sum)
    fill(out, jnp.log2(sums))

    @pl.when(jnp.min(sums) < SMALL)
    def _():
        top = tall
        top[...] = jnp.full_like(top, LOWEST)
        mass[...] = jnp.zeros_like(mass)

        def again(slot, p, t):
            one, two = costs[slot, :, LANES[0]], costs[slot, :, LANES[1]]
            old = top[p]
            new = jnp.maximum(old, jnp.maximum(one, two))
            top[p] = new
            mass[p] = mass[p] * jnp.exp2(old - new) + (jnp.exp2(one - new) + jnp.exp2(two - new))

        for_blocks(codes, targets, again, 1)
        lses = []
        for p in range(tiles):
            for h in range(2):
                tops, masses = top[p, LANES[h], :].T, mass[p, LANES[h], :].T
                peak = jnp.max(tops, axis=0, keepdims=True)
                lses.append(peak + jnp.log2(jnp.sum(masses * jnp.exp2(tops - peak), axis=0, keepdims=True)))
        fill(out, jnp.concatenate(lses, axis=0))


def both(tall):
    return jnp.concatenate([tall, tall], axis=1)


def col_first_kernel(log_ns, held_codes, costs, parts, f, out, peaks, terms, peak, total, tall, codes, sem):
    blocks = Codes(held_codes, codes, sem)
    rows = -log_ns - lse_of(parts_of(parts))
    f[...] = rows
    peak[...] = jnp.full_like(peak, LOWEST)
    total[...] = jnp.zeros_like(total)
    spread_tiles(rows, tall)

    def block(slot, p, t):
        scores = costs[slot] + both(tall[p])
        old = peak[t]
        new = jnp.maximum(old, jnp.max(scores, axis=0, keepdims=True))
        part = jnp.exp2(scores - new)
        terms[slot] = part
        peaks[slot] = new
        peak[t] = new
        total[t] = total[t] * jnp.exp2(old - new) + jnp.sum(part, axis=0, keepdims=True)

    for_blocks(blocks.ready(), out.shape[0], block)
    masses = total[...]
    out[...] = jnp.where(masses > 0.0, peak[...] + jnp.log2(masses), LOWEST)


def row_kernel(first, held_codes, terms, b, given, out, *refs):
    made, _, acc, codes, sem = refs if first else (None, *refs)
    blocks = Codes(held_codes, codes, sem)
    acc[...] = jnp.zeros_like(acc)

    def block(slot, p, t):
        if first:
            factor = jnp.exp2(given[slot] + (b[t] + SHIFT))
            made[slot] = factor
        else:
            factor = given[slot] * b[t]
        for r in range(0, TILE, CHUNK):
            rows = slice(r, r + CHUNK)
            acc[p, rows, :] += (
                terms[slot, rows, LANES[0]] * factor[:, LANES[0]] + terms[slot, rows, LANES[1]] * factor[:, LANES[1]]
            )

    for_blocks(blocks.ready(), b.shape[0], block)
    fill(out, lane_join(acc, jnp.sum))


def col_kernel(ns, last, held_codes, terms, parts, factors, *refs):
    first, out, f, _, acc, tall, codes, sem = refs if last else (None, refs[0], None, *refs[1:])
    blocks = Codes(held_codes, codes, sem)
    a = 1.0 / (ns * total_of(parts_of(parts)))
    spread_tiles(a, tall)
    if last:
        f[...] = (first[...] + (jnp.log2(a) + SHIFT)) * LN2
    acc[...] = jnp.zeros_like(acc)

    def block(slot, p, t):
        sums = [[None] * 2, [None] * 2]
        for r in range(0, TILE, 8):
            factor = tall[p, r : r + 8, :]
            for h in range(2):
                term = terms[slot, r : r + 8, LANES[h]] * factor
                chain = (r // 8) % 2
                sums[h][chain] = term if sums[h][chain] is None else sums[h][chain] + term
        for h in range(2):
            acc[t, :, LANES[h]] += (sums[h][0] + sums[h][1]) * factors[slot, :, LANES[h]]

    for_blocks(blocks.ready(), out.shape[0], block)
    out[...] = jnp.sum(acc[...], axis=1, keepdims=True)


def join_first_kernel(log_nt, parts, g, out):
    g[...] = -log_nt - lse_of(parts_of(parts))
    fill(out, g[...])


def join_kernel(nt, parts, out):
    fill(out, 1.0 / (nt * total_of(parts_of(parts))))


def join_last_kernel(log_nt, parts, g, out):
    fill(out, (g[...] + (-log_nt - jnp.log2(total_of(parts_of(parts))))) * LN2)


def trade_tgt(pieces):
    return lax.all_to_all(pieces, "tgt", 0, 0)


def trade_src(pieces):
    return lax.all_to_all(pieces, "src", 0, 0)


def iterate(x, y, lists, counts, ns, nt, n_src, n_tgt, trade_tgt, trade_src):
    st, tt = x.shape[0] // TILE, y.shape[0] // TILE
    shape = (2 * st, HALF)
    share = (2 * tt // n_src, HALF)
    plain = lambda *shape: jax.ShapeDtypeStruct(shape, jnp.float32)
    scratch = lambda *shape: pltpu.VMEM(shape, jnp.float32)
    row, rows, col, cell, cells = like(shape), like((n_tgt, *shape)), like((tt, 1, TILE)), like(share), like((n_src, *share))
    length = (st * KLOC // HALF + 1) * HALF
    codes = jax.ShapeDtypeStruct((length,), jnp.int32)
    fetch = (pltpu.SMEM((length,), jnp.int32), pltpu.SemaphoreType.DMA((1,)))
    tall, stats = scratch(st, TILE, HALF), scratch(tt, 1, TILE)
    log_ns, log_nt = math.log2(ns), math.log2(nt)
    pieces = lambda v: trade_src(v.reshape((n_src, *share)))
    whole = lambda v: trade_src(v).reshape(tt, 1, TILE)

    blocks = like((st * KLOC, TILE, TILE))
    codes, lse, costs = call(
        row_first_kernel,
        (codes, rows, blocks),
        "svv",
        "hhhh",
        (lists.T, counts, x.T, y.T),
        (
            pltpu.VMEM((E, st * TILE), jnp.bfloat16),
            pltpu.VMEM((E, tt * TILE), jnp.bfloat16),
            pltpu.SMEM((KLOC, st), jnp.int32),
            pltpu.SMEM((st,), jnp.int32),
            pltpu.VMEM((st, TILE, E), jnp.bfloat16),
            tall,
            tall,
            pltpu.SemaphoreType.DMA((4,)),
        ),
        "row_first",
    )
    each = like((st * KLOC, 1, TILE))
    first, lse, peaks, terms = call(
        functools.partial(col_first_kernel, log_ns), (row, col, each, blocks), "vvvv", "vvv", (codes, costs, trade_tgt(lse)),
        (stats, stats, tall, *fetch), "col_first",
    )
    g, share_g = call(functools.partial(join_first_kernel, log_nt), (cell, cells), "vv", "v", (pieces(lse),), (), "join")
    mass, factors, terms = call(
        functools.partial(row_kernel, True), (rows, each), "vv", "vkvv", (codes, terms, whole(share_g), peaks),
        (tall, *fetch), "row_second",
    )
    for iteration in range(1, ITERS):
        last = iteration == ITERS - 1
        mass, *f, terms = call(
            functools.partial(col_kernel, ns, last), (col, plain(*shape)) if last else (col,), "vv" if last else "v",
            "vkvvv" if last else "vkvv", (codes, terms, trade_tgt(mass), factors) + ((first,) if last else ()),
            (scratch(tt, 8, TILE), tall, *fetch), "col",
        )
        if last:
            break
        (b,) = call(functools.partial(join_kernel, nt), (cells,), "v", "v", (pieces(mass),), (), "join")
        mass, terms = call(
            functools.partial(row_kernel, False), (rows,), "v", "vkvv", (codes, terms, whole(b), factors),
            (tall, *fetch), "row",
        )
    (share_g,) = call(functools.partial(join_last_kernel, log_nt), (cells,), "v", "vv", (pieces(mass), g), (), "join")
    return f[0].reshape(-1), trade_src(share_g).reshape(-1)


def local(source_points, target_points, tile_lists, tile_counts):
    n_src, n_tgt = lax.axis_size("src"), lax.axis_size("tgt")
    ns, nt = source_points.shape[0] * n_src, target_points.shape[0] * n_tgt
    return iterate(
        source_points, target_points, tile_lists[:, 0, :], tile_counts[:, 0], ns, nt, n_src, n_tgt, trade_tgt, trade_src
    )


def solution(mesh):
    in_specs = (P("src", None), P("tgt", None), P("src", "tgt", None), P("src", "tgt"))
    out_specs = (P("src"), P("tgt"))
    return jax.shard_map(local, mesh=mesh, in_specs=in_specs, out_specs=out_specs, check_vma=False)
```

time: 182 us -> 185 us (1.016)
  blocking collectives: 155 us -> 158 us
    all_to_all x8, blocking collectives: 117 us -> 120 us  [trade_src(): return lax.all_to_all(pieces, 'src', 0, 0)]
where the time goes in v2:
time: 185 us
  blocking collectives  158 us (85%)
  Pallas kernels  25.6 us (14%)
    all_to_all x8, blocking collectives, trade_src(): return lax.all_to_all(pieces, 'src', 0, 0)  120 us
    all_to_all x4, blocking collectives, trade_tgt(): return lax.all_to_all(pieces, 'tgt', 0, 0)  37.7 us
    pallas_call x12, Pallas kernels, call(): pl.pallas_call(kernel, out_shape=tuple(outs), in_specs=specs_of(specs), o...  25.6 us

profile of v2, /device:TPU:2, one launch (start us, length us, event | category | flops | bytes accessed | tf_op | source)
XLA Modules:
  0.0 184.7 jit_solution(11264903240469328487)
XLA Ops:
  0.6 10.1 %row_first.1 = (s32[128]{0:T(128)S(1)}, f32[8,32,128]{2,1,0:T(8,128)S(1)}, f32[64,256,256]{2,1,0:T(8,128)S(1)}) custom-call(s32[4,16]{1,0:T(4,128)} %bitcast.25, s32[16]{0:T(128)} %bitcast.26, bf16[64,4096]{1,0:T(8,128)(2,1)} %bitcast.23, bf16[64,32768]{1,0:T(8,128)(2,1)} %bitcast.22), custom_call_target="tpu_custom_call" | custom-call | tf_op jit(solution)/shard_map/row_first/pallas_call | solution.py:44
  10.8 11.9 %all_to_all.60.parts = f32[8,32,128]{2,1,0:T(8,128)S(1)} all-to-all(f32[8,32,128]{2,1,0:T(8,128)S(1)} %get-tuple-element.26), channel_id=1, replica_groups=mesh['src'=32,'tgt'=8] {'tgt'}, dimensions={0} | all-to-all | bytes 262144 | tf_op jit(solution)/shard_map/all_to_all | solution.py:286
  22.7 3.1 %col_first.1 = (f32[32,128]{1,0:T(8,128)S(1)}, f32[128,1,256]{2,1,0:T(1,128)S(1)}, f32[64,1,256]{2,1,0:T(1,128)S(1)}, f32[64,256,256]{2,1,0:T(8,128)S(1)}) custom-call(s32[128]{0:T(128)S(1)} %get-tuple-element.24.held_codes, f32[64,256,256]{2,1,0:T(8,128)S(1)} %get-tuple-element.25.costs, f32[8,32,128]{2,1,0:T(8,128)S(1)} %all_to_all.60.parts), custom_call_target="tpu_custom_call" | custom-call | tf_op jit(solution)/shard_map/col_first/pallas_call | solution.py:44
  25.8 22.5 %all_to_all.61.parts = f32[32,8,128]{2,1,0:T(8,128)S(1)} all-to-all(f32[32,8,128]{2,1,0:T(8,128)S(1)} %bitcast.19), channel_id=1, replica_groups=mesh['src'=32,'tgt'=8] {'src'}, dimensions={0} | all-to-all | bytes 262144 | tf_op jit(solution)/shard_map/all_to_all | solution.py:290
  48.2 0.1 join.4
  48.3 13.8 %all_to_all.62 = f32[32,8,128]{2,1,0:T(8,128)S(1)} all-to-all(f32[32,8,128]{2,1,0:T(8,128)S(1)} %get-tuple-element.29), channel_id=1, replica_groups=mesh['src'=32,'tgt'=8] {'src'}, dimensions={0} | all-to-all | bytes 262144 | tf_op jit(solution)/shard_map/all_to_all | solution.py:290
  62.1 2.1 %row_second.1 = (f32[8,32,128]{2,1,0:T(8,128)S(1)}, f32[64,1,256]{2,1,0:T(1,128)S(1)}, f32[64,256,256]{2,1,0:T(8,128)S(1)}) custom-call(s32[128]{0:T(128)S(1)} %get-tuple-element.24.held_codes, f32[64,256,256]{2,1,0:T(8,128)S(1)} %get-tuple-element.27.terms, f32[128,1,256]{2,1,0:T(1,128)S(1)} %bitcast.15, ...), custom_call_target="tpu_custom_call", output_to_operand_aliasing={{2}: (1, {})} | custom-call | tf_op jit(solution)/shard_map/row_second/pallas_call | solution.py:44
  64.2 8.3 %all_to_all.63.parts = f32[8,32,128]{2,1,0:T(8,128)S(1)} all-to-all(f32[8,32,128]{2,1,0:T(8,128)S(1)} %get-tuple-element.32), channel_id=1, replica_groups=mesh['src'=32,'tgt'=8] {'tgt'}, dimensions={0} | all-to-all | bytes 262144 | tf_op jit(solution)/shard_map/all_to_all | solution.py:286
  72.6 1.9 %col.3 = (f32[128,1,256]{2,1,0:T(1,128)S(1)}, f32[64,256,256]{2,1,0:T(8,128)S(1)}) custom-call(s32[128]{0:T(128)S(1)} %get-tuple-element.24.held_codes, f32[64,256,256]{2,1,0:T(8,128)S(1)} %get-tuple-element.31.terms, f32[8,32,128]{2,1,0:T(8,128)S(1)} %all_to_all.63.parts, ...), custom_call_target="tpu_custom_call", output_to_operand_aliasing={{1}: (1, {})} | custom-call | tf_op jit(solution)/shard_map/col/pallas_call | solution.py:44
  74.5 14.2 %all_to_all.64.parts = f32[32,8,128]{2,1,0:T(8,128)S(1)} all-to-all(f32[32,8,128]{2,1,0:T(8,128)S(1)} %bitcast.20), channel_id=1, replica_groups=mesh['src'=32,'tgt'=8] {'src'}, dimensions={0} | all-to-all | bytes 262144 | tf_op jit(solution)/shard_map/all_to_all | solution.py:290
  88.7 14.0 %all_to_all.65 = f32[32,8,128]{2,1,0:T(8,128)S(1)} all-to-all(f32[32,8,128]{2,1,0:T(8,128)S(1)} %join.5), channel_id=1, replica_groups=mesh['src'=32,'tgt'=8] {'src'}, dimensions={0} | all-to-all | bytes 262144 | tf_op jit(solution)/shard_map/all_to_all | solution.py:290
  102.7 2.1 %row.2 = (f32[8,32,128]{2,1,0:T(8,128)S(1)}, f32[64,256,256]{2,1,0:T(8,128)S(1)}) custom-call(s32[128]{0:T(128)S(1)} %get-tuple-element.24.held_codes, f32[64,256,256]{2,1,0:T(8,128)S(1)} %get-tuple-element.34.terms, f32[128,1,256]{2,1,0:T(1,128)S(1)} %bitcast.16, f32[64,1,256]{2,1,0:T(1,128)S(1)} %get-tuple-element.33.factors.given), custom_call_target="tpu_custom_call", output_to_operand_aliasing={{1}: (1, {})} | custom-call | tf_op jit(solution)/shard_map/row/pallas_call | solution.py:44
  104.7 8.7 %all_to_all.66.parts = f32[8,32,128]{2,1,0:T(8,128)S(1)} all-to-all(f32[8,32,128]{2,1,0:T(8,128)S(1)} %get-tuple-element.37), channel_id=1, replica_groups=mesh['src'=32,'tgt'=8] {'tgt'}, dimensions={0} | all-to-all | bytes 262144 | tf_op jit(solution)/shard_map/all_to_all | solution.py:286
  113.4 1.9 %col.4 = (f32[128,1,256]{2,1,0:T(1,128)S(1)}, f32[64,256,256]{2,1,0:T(8,128)S(1)}) custom-call(s32[128]{0:T(128)S(1)} %get-tuple-element.24.held_codes, f32[64,256,256]{2,1,0:T(8,128)S(1)} %get-tuple-element.36.terms, f32[8,32,128]{2,1,0:T(8,128)S(1)} %all_to_all.66.parts, ...), custom_call_target="tpu_custom_call", output_to_operand_aliasing={{1}: (1, {})} | custom-call | tf_op jit(solution)/shard_map/col/pallas_call | solution.py:44
  115.3 13.8 %all_to_all.67.parts = f32[32,8,128]{2,1,0:T(8,128)S(1)} all-to-all(f32[32,8,128]{2,1,0:T(8,128)S(1)} %bitcast.21), channel_id=1, replica_groups=mesh['src'=32,'tgt'=8] {'src'}, dimensions={0} | all-to-all | bytes 262144 | tf_op jit(solution)/shard_map/all_to_all | solution.py:290
  129.1 13.9 %all_to_all.68 = f32[32,8,128]{2,1,0:T(8,128)S(1)} all-to-all(f32[32,8,128]{2,1,0:T(8,128)S(1)} %join.6), channel_id=1, replica_groups=mesh['src'=32,'tgt'=8] {'src'}, dimensions={0} | all-to-all | bytes 262144 | tf_op jit(solution)/shard_map/all_to_all | solution.py:290
  143.0 2.1 %row.3 = (f32[8,32,128]{2,1,0:T(8,128)S(1)}, f32[64,256,256]{2,1,0:T(8,128)S(1)}) custom-call(s32[128]{0:T(128)S(1)} %get-tuple-element.24.held_codes, f32[64,256,256]{2,1,0:T(8,128)S(1)} %get-tuple-element.38.terms, f32[128,1,256]{2,1,0:T(1,128)S(1)} %bitcast.17, f32[64,1,256]{2,1,0:T(1,128)S(1)} %get-tuple-element.33.factors.given), custom_call_target="tpu_custom_call", output_to_operand_aliasing={{1}: (1, {})} | custom-call | tf_op jit(solution)/shard_map/row/pallas_call | solution.py:44
  145.1 8.9 %all_to_all.69.parts = f32[8,32,128]{2,1,0:T(8,128)S(1)} all-to-all(f32[8,32,128]{2,1,0:T(8,128)S(1)} %get-tuple-element.41), channel_id=1, replica_groups=mesh['src'=32,'tgt'=8] {'tgt'}, dimensions={0} | all-to-all | bytes 262144 | tf_op jit(solution)/shard_map/all_to_all | solution.py:286
  153.9 2.2 %col.5 = (f32[128,1,256]{2,1,0:T(1,128)S(1)}, f32[32,128]{1,0:T(8,128)}, f32[64,256,256]{2,1,0:T(8,128)S(1)}) custom-call(s32[128]{0:T(128)S(1)} %get-tuple-element.24.held_codes, f32[64,256,256]{2,1,0:T(8,128)S(1)} %get-tuple-element.40.terms, f32[8,32,128]{2,1,0:T(8,128)S(1)} %all_to_all.69.parts, ...), custom_call_target="tpu_custom_call", output_to_operand_aliasing={{2}: (1, {})} | custom-call | tf_op jit(solution)/shard_map/col/pallas_call | solution.py:44
  156.2 13.9 %all_to_all.70.parts = f32[32,8,128]{2,1,0:T(8,128)S(1)} all-to-all(f32[32,8,128]{2,1,0:T(8,128)S(1)} %bitcast.18), channel_id=1, replica_groups=mesh['src'=32,'tgt'=8] {'src'}, dimensions={0} | all-to-all | bytes 262144 | tf_op jit(solution)/shard_map/all_to_all | solution.py:290
  170.1 13.9 %all_to_all.71 = f32[32,8,128]{2,1,0:T(8,128)S(1)} all-to-all(f32[32,8,128]{2,1,0:T(8,128)S(1)} %join.7), channel_id=1, replica_groups=mesh['src'=32,'tgt'=8] {'src'}, dimensions={0} | all-to-all | bytes 262144 | tf_op jit(solution)/shard_map/all_to_all | solution.py:290
  184.0 0.7 copy.19
  (3 shorter events, 0.1 us)

commit v3 on v2

--- a/solution.py
+++ b/solution.py
@@ -287,7 +287,8 @@
 
 
 def trade_src(pieces):
-    return lax.all_to_all(pieces, "src", 0, 0)
+    order = [y * 8 + z for z in range(8) for y in range(4)]
+    return lax.all_to_all(pieces, "src", 0, 0, axis_index_groups=[order])
 
 
 def iterate(x, y, lists, counts, ns, nt, n_src, n_tgt, trade_tgt, trade_src):

time: 185 us -> 184 us (level)
  no operation moved by 1% of the time
where the time goes in v3:
time: 184 us
  blocking collectives  157 us (85%)
  Pallas kernels  25.2 us (14%)
    all_to_all x8, blocking collectives, trade_src(): return lax.all_to_all(pieces, 'src', 0, 0, axis_index_groups=[order])  120 us
    all_to_all x4, blocking collectives, trade_tgt(): return lax.all_to_all(pieces, 'tgt', 0, 0)  37.5 us
    pallas_call x12, Pallas kernels, call(): pl.pallas_call(kernel, out_shape=tuple(outs), in_specs=specs_of(specs), o...  25.2 us

profile of v3, /device:TPU:2, one launch (start us, length us, event | category | flops | bytes accessed | tf_op | source)
XLA Modules:
  0.0 184.0 jit_solution(8115354549257876848)
XLA Ops:
  0.6 10.3 %row_first.1 = (s32[128]{0:T(128)S(1)}, f32[8,32,128]{2,1,0:T(8,128)S(1)}, f32[64,256,256]{2,1,0:T(8,128)S(1)}) custom-call(s32[4,16]{1,0:T(4,128)} %bitcast.25, s32[16]{0:T(128)} %bitcast.26, bf16[64,4096]{1,0:T(8,128)(2,1)} %bitcast.23, bf16[64,32768]{1,0:T(8,128)(2,1)} %bitcast.22), custom_call_target="tpu_custom_call" | custom-call | tf_op jit(solution)/shard_map/row_first/pallas_call | solution.py:44
  10.9 10.8 %all_to_all.60.parts = f32[8,32,128]{2,1,0:T(8,128)S(1)} all-to-all(f32[8,32,128]{2,1,0:T(8,128)S(1)} %get-tuple-element.26), channel_id=1, replica_groups=mesh['src'=32,'tgt'=8] {'tgt'}, dimensions={0} | all-to-all | bytes 262144 | tf_op jit(solution)/shard_map/all_to_all | solution.py:286
  21.7 2.9 %col_first.1 = (f32[32,128]{1,0:T(8,128)S(1)}, f32[128,1,256]{2,1,0:T(1,128)S(1)}, f32[64,1,256]{2,1,0:T(1,128)S(1)}, f32[64,256,256]{2,1,0:T(8,128)S(1)}) custom-call(s32[128]{0:T(128)S(1)} %get-tuple-element.24.held_codes, f32[64,256,256]{2,1,0:T(8,128)S(1)} %get-tuple-element.25.costs, f32[8,32,128]{2,1,0:T(8,128)S(1)} %all_to_all.60.parts), custom_call_target="tpu_custom_call" | custom-call | tf_op jit(solution)/shard_map/col_first/pallas_call | solution.py:44
  24.6 22.1 %all_to_all.61.parts = f32[32,8,128]{2,1,0:T(8,128)S(1)} all-to-all(f32[32,8,128]{2,1,0:T(8,128)S(1)} %bitcast.19), channel_id=1, replica_groups={{0,64,128,192,8,72,136,200,16,80,144,208,24,88,152,216,32,96,160,224,40..., dimensions={0} | all-to-all | bytes 262144 | tf_op jit(solution)/shard_map/all_to_all | solution.py:291
  46.7 0.1 join.4
  46.8 13.9 %all_to_all.62 = f32[32,8,128]{2,1,0:T(8,128)S(1)} all-to-all(f32[32,8,128]{2,1,0:T(8,128)S(1)} %get-tuple-element.29), channel_id=1, replica_groups={{0,64,128,192,8,72,136,200,16,80,144,208,24,88,152,216,32,96,160,224,40..., dimensions={0} | all-to-all | bytes 262144 | tf_op jit(solution)/shard_map/all_to_all | solution.py:291
  60.7 2.1 %row_second.1 = (f32[8,32,128]{2,1,0:T(8,128)S(1)}, f32[64,1,256]{2,1,0:T(1,128)S(1)}, f32[64,256,256]{2,1,0:T(8,128)S(1)}) custom-call(s32[128]{0:T(128)S(1)} %get-tuple-element.24.held_codes, f32[64,256,256]{2,1,0:T(8,128)S(1)} %get-tuple-element.27.terms, f32[128,1,256]{2,1,0:T(1,128)S(1)} %bitcast.15, ...), custom_call_target="tpu_custom_call", output_to_operand_aliasing={{2}: (1, {})} | custom-call | tf_op jit(solution)/shard_map/row_second/pallas_call | solution.py:44
  62.8 9.0 %all_to_all.63.parts = f32[8,32,128]{2,1,0:T(8,128)S(1)} all-to-all(f32[8,32,128]{2,1,0:T(8,128)S(1)} %get-tuple-element.32), channel_id=1, replica_groups=mesh['src'=32,'tgt'=8] {'tgt'}, dimensions={0} | all-to-all | bytes 262144 | tf_op jit(solution)/shard_map/all_to_all | solution.py:286
  71.8 1.8 col.3
  73.6 14.2 %all_to_all.64.parts = f32[32,8,128]{2,1,0:T(8,128)S(1)} all-to-all(f32[32,8,128]{2,1,0:T(8,128)S(1)} %bitcast.20), channel_id=1, replica_groups={{0,64,128,192,8,72,136,200,16,80,144,208,24,88,152,216,32,96,160,224,40..., dimensions={0} | all-to-all | bytes 262144 | tf_op jit(solution)/shard_map/all_to_all | solution.py:291
  87.8 13.8 %all_to_all.65 = f32[32,8,128]{2,1,0:T(8,128)S(1)} all-to-all(f32[32,8,128]{2,1,0:T(8,128)S(1)} %join.5), channel_id=1, replica_groups={{0,64,128,192,8,72,136,200,16,80,144,208,24,88,152,216,32,96,160,224,40..., dimensions={0} | all-to-all | bytes 262144 | tf_op jit(solution)/shard_map/all_to_all | solution.py:291
  101.6 2.0 %row.2 = (f32[8,32,128]{2,1,0:T(8,128)S(1)}, f32[64,256,256]{2,1,0:T(8,128)S(1)}) custom-call(s32[128]{0:T(128)S(1)} %get-tuple-element.24.held_codes, f32[64,256,256]{2,1,0:T(8,128)S(1)} %get-tuple-element.34.terms, f32[128,1,256]{2,1,0:T(1,128)S(1)} %bitcast.16, f32[64,1,256]{2,1,0:T(1,128)S(1)} %get-tuple-element.33.factors.given), custom_call_target="tpu_custom_call", output_to_operand_aliasing={{1}: (1, {})} | custom-call | tf_op jit(solution)/shard_map/row/pallas_call | solution.py:44
  103.6 8.9 %all_to_all.66.parts = f32[8,32,128]{2,1,0:T(8,128)S(1)} all-to-all(f32[8,32,128]{2,1,0:T(8,128)S(1)} %get-tuple-element.37), channel_id=1, replica_groups=mesh['src'=32,'tgt'=8] {'tgt'}, dimensions={0} | all-to-all | bytes 262144 | tf_op jit(solution)/shard_map/all_to_all | solution.py:286
  112.5 1.8 col.4
  114.3 14.2 %all_to_all.67.parts = f32[32,8,128]{2,1,0:T(8,128)S(1)} all-to-all(f32[32,8,128]{2,1,0:T(8,128)S(1)} %bitcast.21), channel_id=1, replica_groups={{0,64,128,192,8,72,136,200,16,80,144,208,24,88,152,216,32,96,160,224,40..., dimensions={0} | all-to-all | bytes 262144 | tf_op jit(solution)/shard_map/all_to_all | solution.py:291
  128.5 13.8 %all_to_all.68 = f32[32,8,128]{2,1,0:T(8,128)S(1)} all-to-all(f32[32,8,128]{2,1,0:T(8,128)S(1)} %join.6), channel_id=1, replica_groups={{0,64,128,192,8,72,136,200,16,80,144,208,24,88,152,216,32,96,160,224,40..., dimensions={0} | all-to-all | bytes 262144 | tf_op jit(solution)/shard_map/all_to_all | solution.py:291
  142.3 2.0 %row.3 = (f32[8,32,128]{2,1,0:T(8,128)S(1)}, f32[64,256,256]{2,1,0:T(8,128)S(1)}) custom-call(s32[128]{0:T(128)S(1)} %get-tuple-element.24.held_codes, f32[64,256,256]{2,1,0:T(8,128)S(1)} %get-tuple-element.38.terms, f32[128,1,256]{2,1,0:T(1,128)S(1)} %bitcast.17, f32[64,1,256]{2,1,0:T(1,128)S(1)} %get-tuple-element.33.factors.given), custom_call_target="tpu_custom_call", output_to_operand_aliasing={{1}: (1, {})} | custom-call | tf_op jit(solution)/shard_map/row/pallas_call | solution.py:44
  144.3 8.9 %all_to_all.69.parts = f32[8,32,128]{2,1,0:T(8,128)S(1)} all-to-all(f32[8,32,128]{2,1,0:T(8,128)S(1)} %get-tuple-element.41), channel_id=1, replica_groups=mesh['src'=32,'tgt'=8] {'tgt'}, dimensions={0} | all-to-all | bytes 262144 | tf_op jit(solution)/shard_map/all_to_all | solution.py:286
  153.1 2.1 %col.5 = (f32[128,1,256]{2,1,0:T(1,128)S(1)}, f32[32,128]{1,0:T(8,128)}, f32[64,256,256]{2,1,0:T(8,128)S(1)}) custom-call(s32[128]{0:T(128)S(1)} %get-tuple-element.24.held_codes, f32[64,256,256]{2,1,0:T(8,128)S(1)} %get-tuple-element.40.terms, f32[8,32,128]{2,1,0:T(8,128)S(1)} %all_to_all.69.parts, ...), custom_call_target="tpu_custom_call", output_to_operand_aliasing={{2}: (1, {})} | custom-call | tf_op jit(solution)/shard_map/col/pallas_call | solution.py:44
  155.3 14.2 %all_to_all.70.parts = f32[32,8,128]{2,1,0:T(8,128)S(1)} all-to-all(f32[32,8,128]{2,1,0:T(8,128)S(1)} %bitcast.18), channel_id=1, replica_groups={{0,64,128,192,8,72,136,200,16,80,144,208,24,88,152,216,32,96,160,224,40..., dimensions={0} | all-to-all | bytes 262144 | tf_op jit(solution)/shard_map/all_to_all | solution.py:291
  169.5 13.8 %all_to_all.71 = f32[32,8,128]{2,1,0:T(8,128)S(1)} all-to-all(f32[32,8,128]{2,1,0:T(8,128)S(1)} %join.7), channel_id=1, replica_groups={{0,64,128,192,8,72,136,200,16,80,144,208,24,88,152,216,32,96,160,224,40..., dimensions={0} | all-to-all | bytes 262144 | tf_op jit(solution)/shard_map/all_to_all | solution.py:291
  183.3 0.7 copy.19
  (3 shorter events, 0.1 us)

commit v4 on v3

--- a/solution.py
+++ b/solution.py
@@ -219,7 +219,7 @@
         peak[t] = new
         total[t] = total[t] * jnp.exp2(old - new) + jnp.sum(part, axis=0, keepdims=True)
 
-    for_blocks(blocks.ready(), out.shape[0], block)
+    for_blocks(blocks.ready(), out.shape[0], block, 8)
     masses = total[...]
     out[...] = jnp.where(masses > 0.0, peak[...] + jnp.log2(masses), LOWEST)
 
@@ -283,11 +283,12 @@
 
 
 def trade_tgt(pieces):
-    return lax.all_to_all(pieces, "tgt", 0, 0)
+    order = [x * 2 + core for core in range(2) for x in range(4)]
+    return lax.all_to_all(pieces, "tgt", 0, 0, axis_index_groups=[order])
 
 
 def trade_src(pieces):
-    order = [y * 8 + z for z in range(8) for y in range(4)]
+    order = [y * 8 + z for z in (0, 4, 2, 6, 1, 5, 3, 7) for y in (0, 2, 1, 3)]
     return lax.all_to_all(pieces, "src", 0, 0, axis_index_groups=[order])
 
 

time: 184 us -> 184 us (level)
    all_to_all x4, blocking collectives: 37.5 us -> 33.3 us  [trade_tgt(): return lax.all_to_all(pieces, 'tgt', 0, 0, axis_index_groups=[order])]
    all_to_all x8, blocking collectives: 120 us -> 123 us  [trade_src(): return lax.all_to_all(pieces, 'src', 0, 0, axis_index_groups=[order])]
where the time goes in v4:
time: 184 us; the launch traced here: 183 us
  blocking collectives  156 us (85%)
  Pallas kernels  25.5 us (14%)
    all_to_all x8, blocking collectives, trade_src(): return lax.all_to_all(pieces, 'src', 0, 0, axis_index_groups=[order])  123 us
    all_to_all x4, blocking collectives, trade_tgt(): return lax.all_to_all(pieces, 'tgt', 0, 0, axis_index_groups=[order])  33.3 us
    pallas_call x12, Pallas kernels, call(): pl.pallas_call(kernel, out_shape=tuple(outs), in_specs=specs_of(specs), o...  25.5 us

profile of v4, /device:TPU:2, one launch (start us, length us, event | category | flops | bytes accessed | tf_op | source)
XLA Modules:
  0.0 182.8 jit_solution(4363843824374909818)
XLA Ops:
  0.6 10.1 %row_first.1 = (s32[128]{0:T(128)S(1)}, f32[8,32,128]{2,1,0:T(8,128)S(1)}, f32[64,256,256]{2,1,0:T(8,128)S(1)}) custom-call(s32[4,16]{1,0:T(4,128)} %bitcast.25, s32[16]{0:T(128)} %bitcast.26, bf16[64,4096]{1,0:T(8,128)(2,1)} %bitcast.23, bf16[64,32768]{1,0:T(8,128)(2,1)} %bitcast.22), custom_call_target="tpu_custom_call" | custom-call | tf_op jit(solution)/shard_map/row_first/pallas_call | solution.py:44
  10.8 9.0 %all_to_all.60.parts = f32[8,32,128]{2,1,0:T(8,128)S(1)} all-to-all(f32[8,32,128]{2,1,0:T(8,128)S(1)} %get-tuple-element.26), channel_id=1, replica_groups={{0,2,4,6,1,3,5,7},{8,10,12,14,9,11,13,15},{16,18,20,22,17,19,21,23},{24..., dimensions={0} | all-to-all | bytes 262144 | tf_op jit(solution)/shard_map/all_to_all | solution.py:287
  19.8 2.9 %col_first.1 = (f32[32,128]{1,0:T(8,128)S(1)}, f32[128,1,256]{2,1,0:T(1,128)S(1)}, f32[64,1,256]{2,1,0:T(1,128)S(1)}, f32[64,256,256]{2,1,0:T(8,128)S(1)}) custom-call(s32[128]{0:T(128)S(1)} %get-tuple-element.24.held_codes, f32[64,256,256]{2,1,0:T(8,128)S(1)} %get-tuple-element.25.costs, f32[8,32,128]{2,1,0:T(8,128)S(1)} %all_to_all.60.parts), custom_call_target="tpu_custom_call" | custom-call | tf_op jit(solution)/shard_map/col_first/pallas_call | solution.py:44
  22.7 23.5 %all_to_all.61.parts = f32[32,8,128]{2,1,0:T(8,128)S(1)} all-to-all(f32[32,8,128]{2,1,0:T(8,128)S(1)} %bitcast.19), channel_id=1, replica_groups={{0,128,64,192,32,160,96,224,16,144,80,208,48,176,112,240,8,136,72,200,4..., dimensions={0} | all-to-all | bytes 262144 | tf_op jit(solution)/shard_map/all_to_all | solution.py:292
  46.2 0.1 join.4
  46.3 13.8 %all_to_all.62 = f32[32,8,128]{2,1,0:T(8,128)S(1)} all-to-all(f32[32,8,128]{2,1,0:T(8,128)S(1)} %get-tuple-element.29), channel_id=1, replica_groups={{0,128,64,192,32,160,96,224,16,144,80,208,48,176,112,240,8,136,72,200,4..., dimensions={0} | all-to-all | bytes 262144 | tf_op jit(solution)/shard_map/all_to_all | solution.py:292
  60.1 2.1 %row_second.1 = (f32[8,32,128]{2,1,0:T(8,128)S(1)}, f32[64,1,256]{2,1,0:T(1,128)S(1)}, f32[64,256,256]{2,1,0:T(8,128)S(1)}) custom-call(s32[128]{0:T(128)S(1)} %get-tuple-element.24.held_codes, f32[64,256,256]{2,1,0:T(8,128)S(1)} %get-tuple-element.27.terms, f32[128,1,256]{2,1,0:T(1,128)S(1)} %bitcast.15, ...), custom_call_target="tpu_custom_call", output_to_operand_aliasing={{2}: (1, {})} | custom-call | tf_op jit(solution)/shard_map/row_second/pallas_call | solution.py:44
  62.2 8.1 %all_to_all.63.parts = f32[8,32,128]{2,1,0:T(8,128)S(1)} all-to-all(f32[8,32,128]{2,1,0:T(8,128)S(1)} %get-tuple-element.32), channel_id=1, replica_groups={{0,2,4,6,1,3,5,7},{8,10,12,14,9,11,13,15},{16,18,20,22,17,19,21,23},{24..., dimensions={0} | all-to-all | bytes 262144 | tf_op jit(solution)/shard_map/all_to_all | solution.py:287
  70.3 1.9 %col.3 = (f32[128,1,256]{2,1,0:T(1,128)S(1)}, f32[64,256,256]{2,1,0:T(8,128)S(1)}) custom-call(s32[128]{0:T(128)S(1)} %get-tuple-element.24.held_codes, f32[64,256,256]{2,1,0:T(8,128)S(1)} %get-tuple-element.31.terms, f32[8,32,128]{2,1,0:T(8,128)S(1)} %all_to_all.63.parts, ...), custom_call_target="tpu_custom_call", output_to_operand_aliasing={{1}: (1, {})} | custom-call | tf_op jit(solution)/shard_map/col/pallas_call | solution.py:44
  72.2 14.4 %all_to_all.64.parts = f32[32,8,128]{2,1,0:T(8,128)S(1)} all-to-all(f32[32,8,128]{2,1,0:T(8,128)S(1)} %bitcast.20), channel_id=1, replica_groups={{0,128,64,192,32,160,96,224,16,144,80,208,48,176,112,240,8,136,72,200,4..., dimensions={0} | all-to-all | bytes 262144 | tf_op jit(solution)/shard_map/all_to_all | solution.py:292
  86.6 13.9 %all_to_all.65 = f32[32,8,128]{2,1,0:T(8,128)S(1)} all-to-all(f32[32,8,128]{2,1,0:T(8,128)S(1)} %join.5), channel_id=1, replica_groups={{0,128,64,192,32,160,96,224,16,144,80,208,48,176,112,240,8,136,72,200,4..., dimensions={0} | all-to-all | bytes 262144 | tf_op jit(solution)/shard_map/all_to_all | solution.py:292
  100.6 2.1 %row.2 = (f32[8,32,128]{2,1,0:T(8,128)S(1)}, f32[64,256,256]{2,1,0:T(8,128)S(1)}) custom-call(s32[128]{0:T(128)S(1)} %get-tuple-element.24.held_codes, f32[64,256,256]{2,1,0:T(8,128)S(1)} %get-tuple-element.34.terms, f32[128,1,256]{2,1,0:T(1,128)S(1)} %bitcast.16, f32[64,1,256]{2,1,0:T(1,128)S(1)} %get-tuple-element.33.factors.given), custom_call_target="tpu_custom_call", output_to_operand_aliasing={{1}: (1, {})} | custom-call | tf_op jit(solution)/shard_map/row/pallas_call | solution.py:44
  102.6 8.1 %all_to_all.66.parts = f32[8,32,128]{2,1,0:T(8,128)S(1)} all-to-all(f32[8,32,128]{2,1,0:T(8,128)S(1)} %get-tuple-element.37), channel_id=1, replica_groups={{0,2,4,6,1,3,5,7},{8,10,12,14,9,11,13,15},{16,18,20,22,17,19,21,23},{24..., dimensions={0} | all-to-all | bytes 262144 | tf_op jit(solution)/shard_map/all_to_all | solution.py:287
  110.8 1.9 %col.4 = (f32[128,1,256]{2,1,0:T(1,128)S(1)}, f32[64,256,256]{2,1,0:T(8,128)S(1)}) custom-call(s32[128]{0:T(128)S(1)} %get-tuple-element.24.held_codes, f32[64,256,256]{2,1,0:T(8,128)S(1)} %get-tuple-element.36.terms, f32[8,32,128]{2,1,0:T(8,128)S(1)} %all_to_all.66.parts, ...), custom_call_target="tpu_custom_call", output_to_operand_aliasing={{1}: (1, {})} | custom-call | tf_op jit(solution)/shard_map/col/pallas_call | solution.py:44
  112.6 14.6 %all_to_all.67.parts = f32[32,8,128]{2,1,0:T(8,128)S(1)} all-to-all(f32[32,8,128]{2,1,0:T(8,128)S(1)} %bitcast.21), channel_id=1, replica_groups={{0,128,64,192,32,160,96,224,16,144,80,208,48,176,112,240,8,136,72,200,4..., dimensions={0} | all-to-all | bytes 262144 | tf_op jit(solution)/shard_map/all_to_all | solution.py:292
  127.3 13.9 %all_to_all.68 = f32[32,8,128]{2,1,0:T(8,128)S(1)} all-to-all(f32[32,8,128]{2,1,0:T(8,128)S(1)} %join.6), channel_id=1, replica_groups={{0,128,64,192,32,160,96,224,16,144,80,208,48,176,112,240,8,136,72,200,4..., dimensions={0} | all-to-all | bytes 262144 | tf_op jit(solution)/shard_map/all_to_all | solution.py:292
  141.2 2.1 %row.3 = (f32[8,32,128]{2,1,0:T(8,128)S(1)}, f32[64,256,256]{2,1,0:T(8,128)S(1)}) custom-call(s32[128]{0:T(128)S(1)} %get-tuple-element.24.held_codes, f32[64,256,256]{2,1,0:T(8,128)S(1)} %get-tuple-element.38.terms, f32[128,1,256]{2,1,0:T(1,128)S(1)} %bitcast.17, f32[64,1,256]{2,1,0:T(1,128)S(1)} %get-tuple-element.33.factors.given), custom_call_target="tpu_custom_call", output_to_operand_aliasing={{1}: (1, {})} | custom-call | tf_op jit(solution)/shard_map/row/pallas_call | solution.py:44
  143.3 8.1 %all_to_all.69.parts = f32[8,32,128]{2,1,0:T(8,128)S(1)} all-to-all(f32[8,32,128]{2,1,0:T(8,128)S(1)} %get-tuple-element.41), channel_id=1, replica_groups={{0,2,4,6,1,3,5,7},{8,10,12,14,9,11,13,15},{16,18,20,22,17,19,21,23},{24..., dimensions={0} | all-to-all | bytes 262144 | tf_op jit(solution)/shard_map/all_to_all | solution.py:287
  151.3 2.2 %col.5 = (f32[128,1,256]{2,1,0:T(1,128)S(1)}, f32[32,128]{1,0:T(8,128)}, f32[64,256,256]{2,1,0:T(8,128)S(1)}) custom-call(s32[128]{0:T(128)S(1)} %get-tuple-element.24.held_codes, f32[64,256,256]{2,1,0:T(8,128)S(1)} %get-tuple-element.40.terms, f32[8,32,128]{2,1,0:T(8,128)S(1)} %all_to_all.69.parts, ...), custom_call_target="tpu_custom_call", output_to_operand_aliasing={{2}: (1, {})} | custom-call | tf_op jit(solution)/shard_map/col/pallas_call | solution.py:44
  153.5 14.6 %all_to_all.70.parts = f32[32,8,128]{2,1,0:T(8,128)S(1)} all-to-all(f32[32,8,128]{2,1,0:T(8,128)S(1)} %bitcast.18), channel_id=1, replica_groups={{0,128,64,192,32,160,96,224,16,144,80,208,48,176,112,240,8,136,72,200,4..., dimensions={0} | all-to-all | bytes 262144 | tf_op jit(solution)/shard_map/all_to_all | solution.py:292
  168.2 13.9 %all_to_all.71 = f32[32,8,128]{2,1,0:T(8,128)S(1)} all-to-all(f32[32,8,128]{2,1,0:T(8,128)S(1)} %join.7), channel_id=1, replica_groups={{0,128,64,192,32,160,96,224,16,144,80,208,48,176,112,240,8,136,72,200,4..., dimensions={0} | all-to-all | bytes 262144 | tf_op jit(solution)/shard_map/all_to_all | solution.py:292
  182.1 0.7 copy.19
  (3 shorter events, 0.1 us)

commit v5 on v4

--- a/solution.py
+++ b/solution.py
@@ -141,6 +141,7 @@
     copies = [pltpu.make_async_copy(*pair, sems.at[i]) for i, pair in enumerate(pairs)]
     for copy in copies:
         copy.start()
+    mass[...] = jnp.zeros_like(mass)
     copies[0].wait()
     copies[1].wait()
 
@@ -150,7 +151,6 @@
         return n + counts[p]
 
     codes[codes.shape[0] - 1] = lax.fori_loop(0, tiles, listed, 0)
-    mass[...] = jnp.zeros_like(mass)
     copies[2].wait()
     norms = []
     for p in range(tiles):

time: 184 us -> 183 us (level)
  blocking collectives: 156 us -> 151 us
  Pallas kernels: 25.5 us -> 29.7 us
    all_to_all x8, blocking collectives: 123 us -> 118 us  [trade_src(): return lax.all_to_all(pieces, 'src', 0, 0, axis_index_groups=[order])]
    pallas_call x12, Pallas kernels: 25.5 us -> 29.7 us  [call(): pl.pallas_call(kernel, out_shape=tuple(outs), in_specs=specs_of(specs), o...]
where the time goes in v5:
time: 183 us; the launch traced here: 182 us
  blocking collectives  151 us (83%)
  Pallas kernels  29.7 us (16%)
    all_to_all x8, blocking collectives, trade_src(): return lax.all_to_all(pieces, 'src', 0, 0, axis_index_groups=[order])  118 us
    all_to_all x4, blocking collectives, trade_tgt(): return lax.all_to_all(pieces, 'tgt', 0, 0, axis_index_groups=[order])  33.3 us
    pallas_call x12, Pallas kernels, call(): pl.pallas_call(kernel, out_shape=tuple(outs), in_specs=specs_of(specs), o...  29.7 us

profile of v5, /device:TPU:2, one launch (start us, length us, event | category | flops | bytes accessed | tf_op | source)
XLA Modules:
  0.0 182.3 jit_solution(11553007770654814415)
XLA Ops:
  0.6 11.9 %row_first.1 = (s32[128]{0:T(128)S(1)}, f32[8,32,128]{2,1,0:T(8,128)S(1)}, f32[64,256,256]{2,1,0:T(8,128)S(1)}) custom-call(s32[4,16]{1,0:T(4,128)} %bitcast.25, s32[16]{0:T(128)} %bitcast.26, bf16[64,4096]{1,0:T(8,128)(2,1)} %bitcast.23, bf16[64,32768]{1,0:T(8,128)(2,1)} %bitcast.22), custom_call_target="tpu_custom_call" | custom-call | tf_op jit(solution)/shard_map/row_first/pallas_call | solution.py:44
  12.5 9.4 %all_to_all.60.parts = f32[8,32,128]{2,1,0:T(8,128)S(1)} all-to-all(f32[8,32,128]{2,1,0:T(8,128)S(1)} %get-tuple-element.26), channel_id=1, replica_groups={{0,2,4,6,1,3,5,7},{8,10,12,14,9,11,13,15},{16,18,20,22,17,19,21,23},{24..., dimensions={0} | all-to-all | bytes 262144 | tf_op jit(solution)/shard_map/all_to_all | solution.py:287
  21.9 3.6 %col_first.1 = (f32[32,128]{1,0:T(8,128)S(1)}, f32[128,1,256]{2,1,0:T(1,128)S(1)}, f32[64,1,256]{2,1,0:T(1,128)S(1)}, f32[64,256,256]{2,1,0:T(8,128)S(1)}) custom-call(s32[128]{0:T(128)S(1)} %get-tuple-element.24.held_codes, f32[64,256,256]{2,1,0:T(8,128)S(1)} %get-tuple-element.25.costs, f32[8,32,128]{2,1,0:T(8,128)S(1)} %all_to_all.60.parts), custom_call_target="tpu_custom_call" | custom-call | tf_op jit(solution)/shard_map/col_first/pallas_call | solution.py:44
  25.5 19.9 %all_to_all.61.parts = f32[32,8,128]{2,1,0:T(8,128)S(1)} all-to-all(f32[32,8,128]{2,1,0:T(8,128)S(1)} %bitcast.19), channel_id=1, replica_groups={{0,128,64,192,32,160,96,224,16,144,80,208,48,176,112,240,8,136,72,200,4..., dimensions={0} | all-to-all | bytes 262144 | tf_op jit(solution)/shard_map/all_to_all | solution.py:292
  45.4 0.1 join.4
  45.5 14.3 %all_to_all.62 = f32[32,8,128]{2,1,0:T(8,128)S(1)} all-to-all(f32[32,8,128]{2,1,0:T(8,128)S(1)} %get-tuple-element.29), channel_id=1, replica_groups={{0,128,64,192,32,160,96,224,16,144,80,208,48,176,112,240,8,136,72,200,4..., dimensions={0} | all-to-all | bytes 262144 | tf_op jit(solution)/shard_map/all_to_all | solution.py:292
  59.7 2.4 %row_second.1 = (f32[8,32,128]{2,1,0:T(8,128)S(1)}, f32[64,1,256]{2,1,0:T(1,128)S(1)}, f32[64,256,256]{2,1,0:T(8,128)S(1)}) custom-call(s32[128]{0:T(128)S(1)} %get-tuple-element.24.held_codes, f32[64,256,256]{2,1,0:T(8,128)S(1)} %get-tuple-element.27.terms, f32[128,1,256]{2,1,0:T(1,128)S(1)} %bitcast.15, ...), custom_call_target="tpu_custom_call", output_to_operand_aliasing={{2}: (1, {})} | custom-call | tf_op jit(solution)/shard_map/row_second/pallas_call | solution.py:44
  62.2 7.7 %all_to_all.63.parts = f32[8,32,128]{2,1,0:T(8,128)S(1)} all-to-all(f32[8,32,128]{2,1,0:T(8,128)S(1)} %get-tuple-element.32), channel_id=1, replica_groups={{0,2,4,6,1,3,5,7},{8,10,12,14,9,11,13,15},{16,18,20,22,17,19,21,23},{24..., dimensions={0} | all-to-all | bytes 262144 | tf_op jit(solution)/shard_map/all_to_all | solution.py:287
  69.9 2.2 %col.3 = (f32[128,1,256]{2,1,0:T(1,128)S(1)}, f32[64,256,256]{2,1,0:T(8,128)S(1)}) custom-call(s32[128]{0:T(128)S(1)} %get-tuple-element.24.held_codes, f32[64,256,256]{2,1,0:T(8,128)S(1)} %get-tuple-element.31.terms, f32[8,32,128]{2,1,0:T(8,128)S(1)} %all_to_all.63.parts, ...), custom_call_target="tpu_custom_call", output_to_operand_aliasing={{1}: (1, {})} | custom-call | tf_op jit(solution)/shard_map/col/pallas_call | solution.py:44
  72.1 14.2 %all_to_all.64.parts = f32[32,8,128]{2,1,0:T(8,128)S(1)} all-to-all(f32[32,8,128]{2,1,0:T(8,128)S(1)} %bitcast.20), channel_id=1, replica_groups={{0,128,64,192,32,160,96,224,16,144,80,208,48,176,112,240,8,136,72,200,4..., dimensions={0} | all-to-all | bytes 262144 | tf_op jit(solution)/shard_map/all_to_all | solution.py:292
  86.3 13.9 %all_to_all.65 = f32[32,8,128]{2,1,0:T(8,128)S(1)} all-to-all(f32[32,8,128]{2,1,0:T(8,128)S(1)} %join.5), channel_id=1, replica_groups={{0,128,64,192,32,160,96,224,16,144,80,208,48,176,112,240,8,136,72,200,4..., dimensions={0} | all-to-all | bytes 262144 | tf_op jit(solution)/shard_map/all_to_all | solution.py:292
  100.2 2.3 %row.2 = (f32[8,32,128]{2,1,0:T(8,128)S(1)}, f32[64,256,256]{2,1,0:T(8,128)S(1)}) custom-call(s32[128]{0:T(128)S(1)} %get-tuple-element.24.held_codes, f32[64,256,256]{2,1,0:T(8,128)S(1)} %get-tuple-element.34.terms, f32[128,1,256]{2,1,0:T(1,128)S(1)} %bitcast.16, f32[64,1,256]{2,1,0:T(1,128)S(1)} %get-tuple-element.33.factors.given), custom_call_target="tpu_custom_call", output_to_operand_aliasing={{1}: (1, {})} | custom-call | tf_op jit(solution)/shard_map/row/pallas_call | solution.py:44
  102.6 8.1 %all_to_all.66.parts = f32[8,32,128]{2,1,0:T(8,128)S(1)} all-to-all(f32[8,32,128]{2,1,0:T(8,128)S(1)} %get-tuple-element.37), channel_id=1, replica_groups={{0,2,4,6,1,3,5,7},{8,10,12,14,9,11,13,15},{16,18,20,22,17,19,21,23},{24..., dimensions={0} | all-to-all | bytes 262144 | tf_op jit(solution)/shard_map/all_to_all | solution.py:287
  110.7 2.2 %col.4 = (f32[128,1,256]{2,1,0:T(1,128)S(1)}, f32[64,256,256]{2,1,0:T(8,128)S(1)}) custom-call(s32[128]{0:T(128)S(1)} %get-tuple-element.24.held_codes, f32[64,256,256]{2,1,0:T(8,128)S(1)} %get-tuple-element.36.terms, f32[8,32,128]{2,1,0:T(8,128)S(1)} %all_to_all.66.parts, ...), custom_call_target="tpu_custom_call", output_to_operand_aliasing={{1}: (1, {})} | custom-call | tf_op jit(solution)/shard_map/col/pallas_call | solution.py:44
  112.8 13.9 %all_to_all.67.parts = f32[32,8,128]{2,1,0:T(8,128)S(1)} all-to-all(f32[32,8,128]{2,1,0:T(8,128)S(1)} %bitcast.21), channel_id=1, replica_groups={{0,128,64,192,32,160,96,224,16,144,80,208,48,176,112,240,8,136,72,200,4..., dimensions={0} | all-to-all | bytes 262144 | tf_op jit(solution)/shard_map/all_to_all | solution.py:292
  126.8 13.9 %all_to_all.68 = f32[32,8,128]{2,1,0:T(8,128)S(1)} all-to-all(f32[32,8,128]{2,1,0:T(8,128)S(1)} %join.6), channel_id=1, replica_groups={{0,128,64,192,32,160,96,224,16,144,80,208,48,176,112,240,8,136,72,200,4..., dimensions={0} | all-to-all | bytes 262144 | tf_op jit(solution)/shard_map/all_to_all | solution.py:292
  140.7 2.3 %row.3 = (f32[8,32,128]{2,1,0:T(8,128)S(1)}, f32[64,256,256]{2,1,0:T(8,128)S(1)}) custom-call(s32[128]{0:T(128)S(1)} %get-tuple-element.24.held_codes, f32[64,256,256]{2,1,0:T(8,128)S(1)} %get-tuple-element.38.terms, f32[128,1,256]{2,1,0:T(1,128)S(1)} %bitcast.17, f32[64,1,256]{2,1,0:T(1,128)S(1)} %get-tuple-element.33.factors.given), custom_call_target="tpu_custom_call", output_to_operand_aliasing={{1}: (1, {})} | custom-call | tf_op jit(solution)/shard_map/row/pallas_call | solution.py:44
  143.1 8.1 %all_to_all.69.parts = f32[8,32,128]{2,1,0:T(8,128)S(1)} all-to-all(f32[8,32,128]{2,1,0:T(8,128)S(1)} %get-tuple-element.41), channel_id=1, replica_groups={{0,2,4,6,1,3,5,7},{8,10,12,14,9,11,13,15},{16,18,20,22,17,19,21,23},{24..., dimensions={0} | all-to-all | bytes 262144 | tf_op jit(solution)/shard_map/all_to_all | solution.py:287
  151.2 2.5 %col.5 = (f32[128,1,256]{2,1,0:T(1,128)S(1)}, f32[32,128]{1,0:T(8,128)}, f32[64,256,256]{2,1,0:T(8,128)S(1)}) custom-call(s32[128]{0:T(128)S(1)} %get-tuple-element.24.held_codes, f32[64,256,256]{2,1,0:T(8,128)S(1)} %get-tuple-element.40.terms, f32[8,32,128]{2,1,0:T(8,128)S(1)} %all_to_all.69.parts, ...), custom_call_target="tpu_custom_call", output_to_operand_aliasing={{2}: (1, {})} | custom-call | tf_op jit(solution)/shard_map/col/pallas_call | solution.py:44
  153.7 13.9 %all_to_all.70.parts = f32[32,8,128]{2,1,0:T(8,128)S(1)} all-to-all(f32[32,8,128]{2,1,0:T(8,128)S(1)} %bitcast.18), channel_id=1, replica_groups={{0,128,64,192,32,160,96,224,16,144,80,208,48,176,112,240,8,136,72,200,4..., dimensions={0} | all-to-all | bytes 262144 | tf_op jit(solution)/shard_map/all_to_all | solution.py:292
  167.7 13.9 %all_to_all.71 = f32[32,8,128]{2,1,0:T(8,128)S(1)} all-to-all(f32[32,8,128]{2,1,0:T(8,128)S(1)} %join.7), channel_id=1, replica_groups={{0,128,64,192,32,160,96,224,16,144,80,208,48,176,112,240,8,136,72,200,4..., dimensions={0} | all-to-all | bytes 262144 | tf_op jit(solution)/shard_map/all_to_all | solution.py:292
  181.6 0.7 copy.19
  (3 shorter events, 0.1 us)
